TPU v7x, 128 devices: a whole 4x4x4 slice. The times are simulated.
128 devices in a mesh: frame: 8 (over x, z_hi), head: 8 (over y, z_lo), rep: 2 (over core).
Axes of the slice: x: 4, y: 4, z: 4 (z_hi: 2, z_lo: 2; z = z_hi * 2 + z_lo), core: 2. Of those that a mesh axis runs over, the one named last changes fastest.
Arguments:
- tokens: bfloat16 [24576, 3072], P(('rep', 'frame', 'head')), parts along dimension 0, may hold values from -6 to 6
- shift: float32 [3072], replicated, may hold values from -3 to 3
- mod_scale: float32 [3072], replicated, may hold values from -3 to 3
- gate: float32 [3072], replicated, may hold values from -4 to 4
- w_qkv: bfloat16 [3072, 24, 384], P(None, 'head'), may hold values from -0.109375 to 0.109375
- q_gain: float32 [128], replicated, may hold values from 0.1 to 1.9
- k_gain: float32 [128], replicated, may hold values from 0.1 to 1.9
- w_out: bfloat16 [3072, 3072], P('head'), may hold values from -0.109375 to 0.109375
- pattern: int32 [3, 4, 4], replicated, may hold values from 0 to 1, as said below
- counts: int32 [8], replicated, may hold values from 64 to 384, as said below
Outputs:
- mixed: bfloat16 [24576, 3072], P(('rep', 'frame', 'head')), parts along dimension 0
There are 2 independent parts, one for each index of `rep`. A program takes and returns all parts, laid end to end along the dimension named above; an argument that names none is the same for every part. Nothing has to cross between parts.
Inputs may be any that keep to these rules, and one draw needn't show every extreme that they name: Every entry of pattern is 0 or 1; pattern[1, i, i] = 1 for every spatial tile i. counts[t] = 8 * 8 * min(max(V - t * 6, 1), 6) for a number V of valid frames with (6) * 6 + 2 <= V <= 42; tiles past the valid frames keep one frame; non-increasing, the first tile full, the last one holding exactly one frame.
All inputs are finite; a program needn't handle non-finite values.
Results may differ from a plain program's by a relative error of at most 0.011.
Values may be sent and summed in bfloat16 or wider, within the bound.
A program may use at most 192 MiB of HBM per device.

v0:
```python
import jax
import jax.numpy as jnp
from jax import lax
from jax.sharding import PartitionSpec as P

TILE = 384
GS = 4


def padded_2(value, sides, width):
    for axis, dim in sides:
        devices, length = (lax.axis_size(axis), value.shape[dim])
        up = [(i, (i + 1) % devices) for i in range(devices - 1)]
        down = [(j, i) for i, j in up]
        last = lax.slice_in_dim(value, length - width, length, axis=dim)
        leading = lax.slice_in_dim(value, 0, width, axis=dim)
        before = lax.ppermute(last, axis, up)
        after = lax.ppermute(leading, axis, down)
        value = jnp.concatenate([before, value, after], axis=dim)
    return value


def modulate(rows, shift, mod_scale):
    values = rows.astype(jnp.float32)
    center = jnp.mean(values, axis=-1, keepdims=True)
    centred = values - center
    spread = jnp.mean(centred * centred, axis=-1, keepdims=True)
    return (centred * lax.rsqrt(spread + 1e-06) * (1.0 + mod_scale) + shift).astype(jnp.bfloat16)


def head_norm(values, gain):
    square = jnp.mean(values * values, axis=-1, keepdims=True)
    return (values * lax.rsqrt(square + 1e-06) * gain).astype(jnp.bfloat16)


def project(normed, w_qkv, q_gain, k_gain):
    heads = w_qkv.shape[1]
    width = w_qkv.shape[2] // 3
    flat_weight = w_qkv.reshape(w_qkv.shape[0], heads * 3 * width)
    mixing = jnp.dot(normed, flat_weight, preferred_element_type=jnp.float32)
    mixing = mixing.reshape(normed.shape[0], heads, 3, width)
    queries = head_norm(mixing[:, :, 0], q_gain)
    keyset = head_norm(mixing[:, :, 1], k_gain)
    valueset = mixing[:, :, 2].astype(jnp.bfloat16)
    return jnp.stack([queries, keyset, valueset], axis=1)


def tile_attention(query, keyset, valueset, pattern, counts, position):
    spatial = pattern.shape[1]
    rows = query.shape[0]
    tile = rows // spatial
    width = query.shape[1]
    flat_keys = keyset.reshape(3 * rows, width)
    scores = lax.dot_general(
        query, flat_keys, (((1,), (1,)), ((), ())), preferred_element_type=jnp.float32
    )
    scores = (scores * width ** (-0.5)).reshape(spatial, tile, 3, spatial, tile)
    targets = position + jnp.arange(3, dtype=jnp.int32) - 1
    inside = (targets >= 0) & (targets < counts.shape[0])
    matches = targets[:, None] == jnp.arange(counts.shape[0], dtype=jnp.int32)[None, :]
    target_counts = jnp.sum(jnp.where(matches, counts[None, :], 0), axis=1)
    live = inside[:, None] & (jnp.arange(tile, dtype=jnp.int32)[None, :] < target_counts[:, None])
    allowed = jnp.transpose(pattern, (1, 0, 2)) > 0
    maskset = allowed[:, None, :, :, None] & live[None, None, :, None, :]
    scores = jnp.where(maskset, scores, -jnp.inf)
    highest = jnp.max(scores, axis=(2, 3, 4), keepdims=True)
    expo = jnp.exp(scores - highest)
    totals = jnp.sum(expo, axis=(2, 3, 4), keepdims=True)
    weights = (expo / totals).astype(jnp.bfloat16).reshape(rows, 3 * rows)
    flat_values = valueset.reshape(3 * rows, width)
    return jnp.dot(weights, flat_values, preferred_element_type=jnp.float32).astype(jnp.bfloat16)


def per_device(tokens, shift, mod_scale, gate, w_qkv, q_gain, k_gain, w_out, pattern, counts):
    rows = GS * TILE
    local_heads = w_qkv.shape[1]
    width = w_qkv.shape[2] // 3
    normed = modulate(tokens, shift, mod_scale)
    stacked = project(lax.all_gather(normed, "head", axis=0, tiled=True), w_qkv, q_gain, k_gain)
    blocks = stacked.shape[0] // rows
    stacked = stacked.reshape(blocks, rows, 3, local_heads, width)
    keyvals = stacked[:, :, 1:].reshape(blocks, rows, 2 * local_heads * width)
    padded = padded_2(keyvals, (("frame", 0),), 1)
    padded = padded.reshape(blocks + 2, rows, 2, local_heads, width)
    first_tile = lax.axis_index("frame") * blocks

    def one_pair(flat):
        block_index = flat // local_heads
        head_index = flat % local_heads
        query = stacked[block_index, :, 0, head_index]
        window = padded[:, :, :, head_index]
        return tile_attention(
            query, window[:, :, 0], window[:, :, 1], pattern, counts, first_tile + block_index
        )

    outputs = lax.map(one_pair, jnp.arange(blocks * local_heads, dtype=jnp.int32))
    attn = (
        outputs.reshape(blocks, local_heads, rows, width)
        .transpose(0, 2, 1, 3)
        .reshape(blocks * rows, local_heads * width)
    )
    result = lax.psum_scatter(
        jnp.dot(attn, w_out, preferred_element_type=jnp.float32).astype(jnp.bfloat16),
        "head",
        scatter_dimension=0,
        tiled=True,
    ).astype(jnp.float32)
    return (tokens.astype(jnp.float32) + gate * result).astype(jnp.bfloat16)


def solution(mesh):
    placed = (
        P(("rep", "frame", "head"), None),
        P(),
        P(),
        P(),
        P(None, "head", None),
        P(),
        P(),
        P("head", None),
        P(),
        P(),
    )
    return jax.shard_map(
        per_device,
        mesh=mesh,
        in_specs=placed,
        out_specs=P(("rep", "frame", "head"), None),
        check_vma=False,
    )
```

profile of v0, /device:TPU:1, one launch (start us, length us, event | category | flops | bytes accessed | tf_op | source)
XLA Modules:
  0.0 799.9 jit_solution(15431327518123498321)
XLA Ops:
  6.6 1.7 convert_reduce_fusion
  8.2 1.7 fusion.12
  10.0 1.6 fusion.15
  11.6 10.3 %copy.23 = bf16[3072,3,384]{0,2,1:T(8,128)(2,1)} copy(bf16[3072,3,384]{2,0,1:T(8,128)(2,1)} %param.16) | data formatting | bytes 14155776 | tf_op args[4]
  22.0 181.1 %all-gather.2.cloned.1.call-done = bf16[1536,3072]{1,0:T(8,128)(2,1)} async-done(((bf16[192,3072]{1,0:T(8,128)(2,1)}), bf16[1536,3072]{1,0:T(8,128)(2,1)}) %all-gather.2.cloned.1.call-update) | async-done | bytes 9437200 | tf_op jit(solution)/shard_map/all_gather | solution.py:79
  203.0 14.5 %fusion.8 = f32[1536,3,3,128]{0,3,2,1:T(8,128)S(1)} fusion(bf16[3,3,128,3072]{3,2,1,0:T(8,128)(2,1)} %bitcast.90, bf16[1536,3072]{1,0:T(8,128)(2,1)} %all-gather.2.cloned.1.call-done), kind=kOutput, calls=%fused_computation.21 | convolution fusion | flops 10871635968 | bytes 23592960 | tf_op jit(solution)/shard_map/dot_general | solution.py:40
  217.5 0.6 fusion.22
  218.8 0.8 fusion.21
  220.1 1.7 slice.36
  221.8 0.8 copy-done.3
  222.5 5.9 collective-permute-start
  228.5 1.5 collective-permute-start.1
  230.0 97.8 %collective-permute-done = bf16[1,1536,768]{1,2,0:T(8,128)(2,1)} collective-permute-done((bf16[1,1536,768]{1,2,0:T(8,128)(2,1)}, bf16[1,1536,768]{1,2,0:T(8,128)(2,1)}, u32[]{:S(2)}, u32[]{:S(2)}) %collective-permute-start) | collective-permute-done | bytes 2359328 | tf_op jit(solution)/shard_map/ppermute | solution.py:17
  327.8 6.5 pad_maximum_fusion
  334.2 251.8 %while.13 = (s32[]{:T(128)}, bf16[3,1536,128]{1,2,0:T(8,128)(2,1)}, s32[3,4,4]{2,0,1:T(4,128)S(1)}, s32[3]{0:T(128)S(1)}, s32[]{:T(128)}, /*index=5*/s32[8]{0:T(...) while((s32[]{:T(128)}, bf16[3,1536,128]{1,2,0:T(8,128)(2,1)}, ...), condition=%wide.region_8.9_spmd, body=%wide.region_4.8_spmd.sunk | while | flops 3680716288 | bytes 132191672 | solution.py:96
  334.3 0.6 dynamic_slice.35
  337.2 5.0 broadcast_in_dim.75
  342.2 27.6 %broadcast_in_dim.76 = pred[1536,4608]{1,0:T(32,128)(4,1)} reshape(pred[4,384,3,4,384]{4,3,2,1,0:T(4,128)(4,1)} %broadcast_in_dim.75) | data formatting | bytes 14155776 | tf_op jit(solution)/shard_map/while/body/eval_jaxpr/jit(_where)/broadcast_in_dim | solution.py:65
  369.8 3.3 constant_dynamic-slice_fusion.2
  373.1 4.3 copy.39
  377.4 1.8 fusion.40
  379.1 14.2 %fusion.42 = (f32[1536]{0:T(1024)S(1)}, f32[1536,4608]{1,0:T(8,128)}) fusion(pred[1536,4608]{1,0:T(32,128)(4,1)} %broadcast_in_dim.76, bf16[4608,128]{1,0:T(8,128)(2,1)S(1)} %bitcast.88, bf16[1,1536,3,3,128]{1,4,3,2,0:T(8,128)(2,1)} %get-tuple-element.279, s32[]{:T(128)S(6)} %select_n.59), kind=kOutput, calls=%fused_computation.53.clone.1 | convolution fusion | flops 1833171456 | bytes 36968452 | tf_op jit(solution)/shard_map/while/body/eval_jaxpr/dot_general | solution.py:54
  393.4 12.3 %fusion.43 = f32[1536]{0:T(1024)S(1)} fusion(f32[1536,4608]{1,0:T(8,128)} %get-tuple-element.243, f32[1536]{0:T(1024)S(1)} %get-tuple-element.244), kind=kLoop, calls=%fused_computation.3.clone.1 | loop fusion | flops 14154240 | bytes 28323840 | tf_op jit(solution)/shard_map/while/body/eval_jaxpr/reduce_sum | solution.py:68
  405.7 11.5 %fusion.44 = bf16[1,1536,128]{2,1,0:T(8,128)(2,1)S(1)} fusion(bf16[4608,128]{1,0:T(8,128)(2,1)S(1)} %bitcast.89, f32[1536,4608]{1,0:T(8,128)} %get-tuple-element.243, f32[1536]{0:T(1024)S(1)} %fusion.43, f32[1536]{0:T(1024)S(1)} %get-tuple-element.244), kind=kOutput, calls=%fused_computation.6.clone.1 | convolution fusion | flops 1833369600 | bytes 29896704 | tf_op jit(solution)/shard_map/while/body/eval_jaxpr/dot_general | solution.py:71
  417.4 0.8 constant_dynamic-update-slice_fusion.2
  418.2 0.6 dynamic_slice.35
  421.1 5.0 broadcast_in_dim.75
  426.1 27.6 %broadcast_in_dim.76 = pred[1536,4608]{1,0:T(32,128)(4,1)} reshape(pred[4,384,3,4,384]{4,3,2,1,0:T(4,128)(4,1)} %broadcast_in_dim.75) | data formatting | bytes 14155776 | tf_op jit(solution)/shard_map/while/body/eval_jaxpr/jit(_where)/broadcast_in_dim | solution.py:65
  453.7 3.3 constant_dynamic-slice_fusion.2
  457.0 4.3 copy.39
  461.3 1.8 fusion.40
  463.1 14.2 %fusion.42 = (f32[1536]{0:T(1024)S(1)}, f32[1536,4608]{1,0:T(8,128)}) fusion(pred[1536,4608]{1,0:T(32,128)(4,1)} %broadcast_in_dim.76, bf16[4608,128]{1,0:T(8,128)(2,1)S(1)} %bitcast.88, bf16[1,1536,3,3,128]{1,4,3,2,0:T(8,128)(2,1)} %get-tuple-element.279, s32[]{:T(128)S(6)} %select_n.59), kind=kOutput, calls=%fused_computation.53.clone.1 | convolution fusion | flops 1833171456 | bytes 36968452 | tf_op jit(solution)/shard_map/while/body/eval_jaxpr/dot_general | solution.py:54
  477.3 12.3 %fusion.43 = f32[1536]{0:T(1024)S(1)} fusion(f32[1536,4608]{1,0:T(8,128)} %get-tuple-element.243, f32[1536]{0:T(1024)S(1)} %get-tuple-element.244), kind=kLoop, calls=%fused_computation.3.clone.1 | loop fusion | flops 14154240 | bytes 28323840 | tf_op jit(solution)/shard_map/while/body/eval_jaxpr/reduce_sum | solution.py:68
  489.6 11.5 %fusion.44 = bf16[1,1536,128]{2,1,0:T(8,128)(2,1)S(1)} fusion(bf16[4608,128]{1,0:T(8,128)(2,1)S(1)} %bitcast.89, f32[1536,4608]{1,0:T(8,128)} %get-tuple-element.243, f32[1536]{0:T(1024)S(1)} %fusion.43, f32[1536]{0:T(1024)S(1)} %get-tuple-element.244), kind=kOutput, calls=%fused_computation.6.clone.1 | convolution fusion | flops 1833369600 | bytes 29896704 | tf_op jit(solution)/shard_map/while/body/eval_jaxpr/dot_general | solution.py:71
  501.3 0.8 constant_dynamic-update-slice_fusion.2
  502.1 0.6 dynamic_slice.35
  505.0 5.0 broadcast_in_dim.75
  510.0 27.6 %broadcast_in_dim.76 = pred[1536,4608]{1,0:T(32,128)(4,1)} reshape(pred[4,384,3,4,384]{4,3,2,1,0:T(4,128)(4,1)} %broadcast_in_dim.75) | data formatting | bytes 14155776 | tf_op jit(solution)/shard_map/while/body/eval_jaxpr/jit(_where)/broadcast_in_dim | solution.py:65
  537.6 3.3 constant_dynamic-slice_fusion.2
  541.0 4.3 copy.39
  545.2 1.8 fusion.40
  547.0 14.2 %fusion.42 = (f32[1536]{0:T(1024)S(1)}, f32[1536,4608]{1,0:T(8,128)}) fusion(pred[1536,4608]{1,0:T(32,128)(4,1)} %broadcast_in_dim.76, bf16[4608,128]{1,0:T(8,128)(2,1)S(1)} %bitcast.88, bf16[1,1536,3,3,128]{1,4,3,2,0:T(8,128)(2,1)} %get-tuple-element.279, s32[]{:T(128)S(6)} %select_n.59), kind=kOutput, calls=%fused_computation.53.clone.1 | convolution fusion | flops 1833171456 | bytes 36968452 | tf_op jit(solution)/shard_map/while/body/eval_jaxpr/dot_general | solution.py:54
  561.2 12.3 %fusion.43 = f32[1536]{0:T(1024)S(1)} fusion(f32[1536,4608]{1,0:T(8,128)} %get-tuple-element.243, f32[1536]{0:T(1024)S(1)} %get-tuple-element.244), kind=kLoop, calls=%fused_computation.3.clone.1 | loop fusion | flops 14154240 | bytes 28323840 | tf_op jit(solution)/shard_map/while/body/eval_jaxpr/reduce_sum | solution.py:68
  573.6 11.5 %fusion.44 = bf16[1,1536,128]{2,1,0:T(8,128)(2,1)S(1)} fusion(bf16[4608,128]{1,0:T(8,128)(2,1)S(1)} %bitcast.89, f32[1536,4608]{1,0:T(8,128)} %get-tuple-element.243, f32[1536]{0:T(1024)S(1)} %fusion.43, f32[1536]{0:T(1024)S(1)} %get-tuple-element.244), kind=kOutput, calls=%fused_computation.6.clone.1 | convolution fusion | flops 1833369600 | bytes 29896704 | tf_op jit(solution)/shard_map/while/body/eval_jaxpr/dot_general | solution.py:71
  585.3 0.8 constant_dynamic-update-slice_fusion.2
  586.1 9.0 %convolution_convert_fusion = bf16[1536,3072]{1,0:T(8,128)(2,1)} fusion(bf16[1536,384]{0,1:T(8,128)(2,1)} %bitcast.91, bf16[384,3072]{1,0:T(8,128)(2,1)S(1)} %copy-done), kind=kOutput, calls=%fused_computation.20 | convolution fusion | flops 3628597248 | bytes 12976128 | tf_op jit(solution)/shard_map/dot_general | solution.py:103
  595.1 195.3 %reduce-scatter.2.cloned.1.call-done = bf16[192,3072]{1,0:T(8,128)(2,1)} async-done(((bf16[1536,3072]{1,0:T(8,128)(2,1)}), bf16[192,3072]{1,0:T(8,128)(2,1)}) %reduce-scatter.2.cloned.1.call-update) | async-done | bytes 1179664 | tf_op jit(solution)/shard_map/reduce_scatter | solution.py:102
  790.4 2.7 fusion.16
  (56 shorter events, 2.9 us)
Async XLA Ops:
  6.5 579.5 %copy-start = (bf16[384,3072]{1,0:T(8,128)(2,1)S(1)}, bf16[384,3072]{1,0:T(8,128)(2,1)}, u32[]{:S(2)}) copy-start(bf16[384,3072]{1,0:T(8,128)(2,1)} %param.19) | copy-start | bytes 7077892
  6.5 3.5 copy-start.1
  6.5 3.5 copy-start.4
  6.5 196.5 %all-gather.2.cloned.1.call-start = ((), (), s32[]{:S(2)}) async-start(), calls=%async_computation.1 | async-start | bytes 10616832 | tf_op jit(solution)/shard_map/all_gather | solution.py:79
  6.5 3.4 copy-start.5
  11.6 778.8 %reduce-scatter.2.cloned.1.call-start = ((), (), s32[]{:S(2)}) async-start(), calls=%async_computation.2 | async-start | bytes 10616832 | tf_op jit(solution)/shard_map/reduce_scatter | solution.py:102
  218.1 0.7 copy-start.8
  218.1 0.7 copy-start.9
  220.1 2.5 copy-start.3
  220.1 9.9 %copy-start.7 = (s32[3,4,4]{2,1,0:T(4,128)S(1)}, s32[3,4,4]{2,1,0:T(4,128)}, u32[]{:S(2)}) copy-start(s32[3,4,4]{2,1,0:T(4,128)} %param.20) | copy-start | bytes 580
  222.5 105.2 %collective-permute-start = (bf16[1,1536,768]{1,2,0:T(8,128)(2,1)}, bf16[1,1536,768]{1,2,0:T(8,128)(2,1)}, u32[]{:S(2)}, u32[]{:S(2)}) collective-permute-start(bf16[1,1536,768]{1,2,0:T(8,128)(2,1)} %bitcast.18), channel_id=1, source_target_pairs={{0,16},{16,32},{32,48},{48,64},{64,80},{80,96},{96,112},{1,17},{17... | collective-permute-start | bytes 7077896 | tf_op jit(solution)/shard_map/ppermute | solution.py:17
  228.5 99.3 %collective-permute-start.1 = (bf16[1,1536,768]{1,2,0:T(8,128)(2,1)}, bf16[1,1536,768]{1,2,0:T(8,128)(2,1)}, u32[]{:S(2)}, u32[]{:S(2)}) collective-permute-start(bf16[1,1536,768]{1,2,0:T(8,128)(2,1)} %bitcast.18), channel_id=1, source_target_pairs={{16,0},{32,16},{48,32},{64,48},{80,64},{96,80},{112,96},{17,1},{33... | collective-permute-start | bytes 7077896 | tf_op jit(solution)/shard_map/ppermute | solution.py:18
  327.8 6.5 copy-start.10
  595.1 195.3 %copy-start.2 = (bf16[192,3072]{1,0:T(8,128)(2,1)S(1)}, bf16[192,3072]{1,0:T(8,128)(2,1)}, u32[]{:S(2)}) copy-start(bf16[192,3072]{1,0:T(8,128)(2,1)} %param.12) | copy-start | bytes 3538948
  595.1 195.3 %copy-start.6 = (f32[3072]{0:T(1024)S(1)}, f32[3072]{0:T(1024)}, u32[]{:S(2)}) copy-start(f32[3072]{0:T(1024)} %param.15) | copy-start | bytes 36868
Sparse Core Ops, SparseCore 0:
  11.7 191.2 all-gather.1
  595.2 195.1 reduce-scatter.1
where the time goes:
time: 803 us; the launch traced here: 800 us
  waiting for transfers between devices  474 us (59%)
  local copies, waits for them, and re-layouts  144 us (18%)
  matrix products  101 us (13%)
  other arithmetic  54 us (7%)
  between operations  13.6 us (2%)
    reduce_scatter x1, waiting for transfers between devices, per_device(): lax.psum_scatter(jnp.dot(attn, w_out, preferred_element_type=jnp.float32)...  195 us
    all_gather x1, waiting for transfers between devices, per_device(): lax.all_gather(normed, 'head', axis=0, tiled=True)  181 us
    ppermute x1, waiting for transfers between devices, padded_2(): before = lax.ppermute(last, axis, up)  97.8 us
    broadcast_in_dim x6, local copies, waits for them, and re-layouts, tile_attention(): scores = jnp.where(maskset, scores, -jnp.inf)  97.7 us
    dot_general x3, matrix products, tile_attention(): lax.dot_general(query, flat_keys, (((1,), (1,)), ((), ())), preferred_ele...  42.7 us
    reduce_sum x3, other arithmetic, tile_attention(): totals = jnp.sum(expo, axis=(2, 3, 4), keepdims=True)  36.9 us
    dot_general x3, matrix products, tile_attention(): jnp.dot(weights, flat_values, preferred_element_type=jnp.float32)  34.5 us
    dynamic_slice x6, local copies, waits for them, and re-layouts, one_pair(): window = padded[:, :, :, head_index]  22.8 us
  transfers between devices with their start and end apart: 4, of which 3 were waited for; matrix products, arithmetic and copies ran while one was open for 1% of the time, Pallas kernels for 0%

commit v1 on v0

v1 whole, which is shorter than its diff:
```python
import functools

import jax
import jax.numpy as jnp
from jax import lax
from jax.experimental import pallas as pl
from jax.experimental.pallas import tpu as pltpu
from jax.sharding import PartitionSpec as P

TILE = 384
GS = 4
HD = 128
NT = 8
ROWS = GS * TILE
VMEM_LIMIT = 56 * 1024 * 1024
QSCALE = HD**-0.5 * 1.4426950408889634


def modulate(rows, shift, mod_scale):
    values = rows.astype(jnp.float32)
    center = jnp.mean(values, axis=-1, keepdims=True)
    centred = values - center
    spread = jnp.mean(centred * centred, axis=-1, keepdims=True)
    return (centred * lax.rsqrt(spread + 1e-06) * (1.0 + mod_scale) + shift).astype(jnp.bfloat16)


def head_norm(values, gain):
    square = jnp.mean(values * values, axis=-1, keepdims=True)
    return (values * lax.rsqrt(square + 1e-06) * gain).astype(jnp.bfloat16)


def project_kernel(x_ref, w_ref, qg_ref, kg_ref, q_ref, kv_ref):
    x = x_ref[...]
    heads = w_ref.shape[0]
    for h in range(heads):
        mixed = jnp.dot(x, w_ref[h], preferred_element_type=jnp.float32)
        q_ref[:, h * HD : (h + 1) * HD] = head_norm(mixed[:, :HD], qg_ref[...])
        kv_ref[:, h * HD : (h + 1) * HD] = head_norm(mixed[:, HD : 2 * HD], kg_ref[...])
        kv_ref[:, (heads + h) * HD : (heads + h + 1) * HD] = mixed[:, 2 * HD :].astype(jnp.bfloat16)


def project(normed, w, q_gain, k_gain):
    heads, depth, width = w.shape
    rows = normed.shape[0]
    step = 192
    return pl.pallas_call(
        project_kernel,
        name="project",
        grid=(rows // step,),
        out_shape=(
            jax.ShapeDtypeStruct((rows, heads * HD), jnp.bfloat16),
            jax.ShapeDtypeStruct((rows, 2 * heads * HD), jnp.bfloat16),
        ),
        in_specs=[
            pl.BlockSpec((step, depth), lambda i: (i, 0)),
            pl.BlockSpec((heads, depth, width), lambda i: (0, 0, 0), pipeline_mode=pl.Buffered(1)),
            pl.BlockSpec((1, HD), lambda i: (0, 0)),
            pl.BlockSpec((1, HD), lambda i: (0, 0)),
        ],
        out_specs=(
            pl.BlockSpec((step, heads * HD), lambda i: (i, 0)),
            pl.BlockSpec((step, 2 * heads * HD), lambda i: (i, 0)),
        ),
        compiler_params=pltpu.CompilerParams(vmem_limit_bytes=VMEM_LIMIT),
    )(normed, w, (q_gain * QSCALE)[None], k_gain[None])


def attention_kernel(heads, pat_ref, cnt_ref, t_ref, q_ref, a_ref, b_ref, c_ref, out_ref, kwin, vwin, vext, acc, todo, sem):
    t = t_ref[0]
    width = heads * HD
    windows = (a_ref, b_ref, c_ref)
    copies = []
    for o in range(3):
        for part, into in ((0, kwin), (1, vwin)):
            copy = pltpu.make_async_copy(
                windows[o].at[:, part * width : (part + 1) * width], into.at[o], sem.at[2 * o + part]
            )
            copy.start()
            copies.append(copy)

    def list_tile(i, carry):
        count = jnp.int32(0)
        for o in range(3):
            inside = (t + o - 1 >= 0) & (t + o - 1 < NT)
            for j in range(GS):
                todo[i * 13 + 1 + count] = o * GS + j
                live = inside & (pat_ref[(o * GS + i) * GS + j] > 0)
                count = count + live.astype(jnp.int32)
        todo[i * 13] = count
        return carry

    lax.fori_loop(0, GS, list_tile, 0)
    for copy in copies:
        copy.wait()

    place = lax.broadcasted_iota(jnp.int32, (TILE, HD), 0)
    for o in range(3):
        valid = cnt_ref[jnp.clip(t + o - 1, 0, NT - 1)]
        keep = place < valid
        ones = jnp.where(keep, 1.0, 0.0).astype(jnp.bfloat16)

        def fill(j, carry):
            rows = pl.ds(pl.multiple_of(j * TILE, TILE), TILE)
            for h in range(heads):
                vext[o, rows, 2 * h * HD : (2 * h + 1) * HD] = (
                    vwin[o, rows, h * HD : (h + 1) * HD] * ones
                )
                vext[o, rows, (2 * h + 1) * HD : (2 * h + 2) * HD] = ones
            return carry

        lax.fori_loop(0, GS, fill, 0)

    def tile(i, carry):
        mine = pl.ds(pl.multiple_of(i * TILE, TILE), TILE)
        acc[...] = jnp.zeros_like(acc)

        def pair(n, carry):
            which = todo[i * 13 + 1 + n]
            o = which // GS
            keys = pl.ds(pl.multiple_of((which % GS) * TILE, TILE), TILE)
            for h in range(heads):
                score = lax.dot_general(
                    q_ref[mine, h * HD : (h + 1) * HD],
                    kwin[o, keys, h * HD : (h + 1) * HD],
                    (((1,), (1,)), ((), ())),
                    preferred_element_type=jnp.float32,
                )
                prob = jnp.exp2(score).astype(jnp.bfloat16)
                acc[h] += jnp.dot(
                    prob, vext[o, keys, 2 * h * HD : (2 * h + 2) * HD], preferred_element_type=jnp.float32
                )
            return carry

        lax.fori_loop(0, todo[i * 13], pair, 0)
        for h in range(heads):
            out_ref[mine, h * HD : (h + 1) * HD] = (acc[h, :, :HD] / acc[h, :, HD:]).astype(jnp.bfloat16)
        return carry

    lax.fori_loop(0, GS, tile, 0)


def attention(q, before, own, after, pattern, counts, t):
    rows, width = q.shape
    heads = width // HD
    smem = pl.BlockSpec(memory_space=pltpu.SMEM)
    hbm = pl.BlockSpec(memory_space=pl.ANY)
    vmem = pl.BlockSpec(memory_space=pltpu.VMEM)
    return pl.pallas_call(
        functools.partial(attention_kernel, heads),
        name="attention",
        out_shape=jax.ShapeDtypeStruct((rows, width), jnp.bfloat16),
        in_specs=[smem, smem, smem, vmem, hbm, hbm, hbm],
        out_specs=vmem,
        scratch_shapes=[
            pltpu.VMEM((3, rows, width), jnp.bfloat16),
            pltpu.VMEM((3, rows, width), jnp.bfloat16),
            pltpu.VMEM((3, rows, 2 * width), jnp.bfloat16),
            pltpu.VMEM((heads, TILE, 2 * HD), jnp.float32),
            pltpu.SMEM((GS * 13 + 4,), jnp.int32),
            pltpu.SemaphoreType.DMA((6,)),
        ],
        compiler_params=pltpu.CompilerParams(vmem_limit_bytes=VMEM_LIMIT),
    )(pattern.reshape(-1), counts, t.reshape(1), q, before, own, after)


def per_device(tokens, shift, mod_scale, gate, w_qkv, q_gain, k_gain, w_out, pattern, counts):
    normed = modulate(tokens, shift, mod_scale)
    gathered = lax.all_gather(normed, "head", axis=0, tiled=True)
    q, kv = project(gathered, jnp.transpose(w_qkv, (1, 0, 2)), q_gain, k_gain)
    size = lax.axis_size("frame")
    up = [(i, (i + 1) % size) for i in range(size - 1)]
    down = [(j, i) for i, j in up]
    before = lax.ppermute(kv, "frame", up)
    after = lax.ppermute(kv, "frame", down)
    attn = attention(q, before, kv, after, pattern, counts, lax.axis_index("frame"))
    result = lax.psum_scatter(
        jnp.dot(attn, w_out, preferred_element_type=jnp.float32).astype(jnp.bfloat16),
        "head",
        scatter_dimension=0,
        tiled=True,
    ).astype(jnp.float32)
    return (tokens.astype(jnp.float32) + gate * result).astype(jnp.bfloat16)


def solution(mesh):
    placed = (
        P(("rep", "frame", "head"), None),
        P(),
        P(),
        P(),
        P(None, "head", None),
        P(),
        P(),
        P("head", None),
        P(),
        P(),
    )
    return jax.shard_map(
        per_device,
        mesh=mesh,
        in_specs=placed,
        out_specs=P(("rep", "frame", "head"), None),
        check_vma=False,
    )
```

time: 803 us -> 574 us (0.71)
  local copies, waits for them, and re-layouts: 144 us -> 0.7 us
  matrix products: 101 us -> 8.96 us
  other arithmetic: 54 us -> 8.26 us
  Pallas kernels: 0 us -> 44.7 us
  waiting for transfers between devices: 474 us -> 490 us
    broadcast_in_dim x6 -> x0, local copies, waits for them, and re-layouts: 97.7 us -> none  [tile_attention(): scores = jnp.where(maskset, scores, -jnp.inf)]
    dot_general x7 -> x0, matrix products: 91.8 us -> none  [the longest x3 42.7 us: tile_attention(): lax.dot_general(query, flat_keys, (((1,), (1,)), ((), ())), preferred_ele...]
    pallas_call x0 -> x2, Pallas kernels: none -> 44.7 us  [the longest x1 23.7 us: attention(): pl.pallas_call(functools.partial(attention_kernel, heads), name='attentio...]
    reduce_sum x7 -> x0, other arithmetic: 38.1 us -> none  [the longest x3 36.9 us: tile_attention(): totals = jnp.sum(expo, axis=(2, 3, 4), keepdims=True)]
    dynamic_slice x9 -> x0, local copies, waits for them, and re-layouts: 24.6 us -> none  [the longest x6 22.8 us: one_pair(): window = padded[:, :, :, head_index]]
    unnamed x23 -> x14, local copies, waits for them, and re-layouts: 11.6 us -> 0.03 us
    all_gather x1, waiting for transfers between devices: 181 us -> 191 us  [per_device(): gathered = lax.all_gather(normed, 'head', axis=0, tiled=True)]
  transfers between devices with their start and end apart: 4 -> 4, of which waited for: 3 -> 3; matrix products, arithmetic and copies ran while one was open for 1% -> 0% of each run, Pallas kernels for 0% -> 0%
where the time goes in v1:
time: 574 us
  waiting for transfers between devices  490 us (85%)
  Pallas kernels  44.7 us (8%)
  between operations  13.5 us (2%)
  matrix products  8.96 us (2%)
  other arithmetic  8.26 us (1%)
  starting transfers between devices  7.21 us (1%)
    reduce_scatter x1, waiting for transfers between devices, per_device(): lax.psum_scatter(jnp.dot(attn, w_out, preferred_element_type=jnp.float32)...  202 us
    all_gather x1, waiting for transfers between devices, per_device(): gathered = lax.all_gather(normed, 'head', axis=0, tiled=True)  191 us
    ppermute x1, waiting for transfers between devices, per_device(): before = lax.ppermute(kv, 'frame', up)  97.4 us
    pallas_call x1, Pallas kernels, attention(): pl.pallas_call(functools.partial(attention_kernel, heads), name='attentio...  23.7 us
    pallas_call x1, Pallas kernels, project(): pl.pallas_call(project_kernel, name='project', grid=(rows // step,), out_...  21 us
  transfers between devices with their start and end apart: 4, of which 3 were waited for; matrix products, arithmetic and copies ran while one was open for 0% of the time, Pallas kernels for 0%

profile of v1, /device:TPU:1, one launch (start us, length us, event | category | flops | bytes accessed | tf_op | source)
XLA Modules:
  0.0 573.7 jit_solution(737844555311902218)
XLA Ops:
  6.5 0.0 copy-start
  6.5 0.0 copy-start.1
  6.5 0.0 copy-start.2
  6.5 0.0 all-gather.2.cloned.1.call-start
  6.5 0.0 copy-start.3
  6.6 1.7 convert_reduce_fusion
  8.2 0.0 copy-start.6
  8.2 1.7 fusion.2
  10.0 0.0 copy-done.3
  10.0 0.0 copy-done.1
  10.0 0.0 copy-done.2
  10.0 1.6 fusion.5
  11.6 0.0 all-gather.2.cloned.1.call-update
  11.6 0.0 reduce-scatter.2.cloned.1.call-start
  11.7 0.0 copy-done.6
  11.7 0.6 multiply_bitcast_fusion.qg_ref
  12.2 190.8 %all-gather.2.cloned.1.call-done.x_ref = bf16[1536,3072]{1,0:T(8,128)(2,1)} async-done(((bf16[192,3072]{1,0:T(8,128)(2,1)}), bf16[1536,3072]{1,0:T(8,128)(2,1)}) %all-gather.2.cloned.1.call-update) | async-done | bytes 9437200 | tf_op jit(solution)/shard_map/all_gather | solution.py:168
  203.0 0.0 copy-start.5
  203.0 21.0 %project.1 = (bf16[1536,384]{1,0:T(8,128)(2,1)}, bf16[1536,768]{1,0:T(8,128)(2,1)}) custom-call(bf16[1536,3072]{1,0:T(8,128)(2,1)} %all-gather.2.cloned.1.call-done.x_ref, bf16[3,3072,384]{2,1,0:T(8,128)(2,1)} %bitcast.7, f32[1,128]{1,0:T(1,128)} %multiply_bitcast_fusion.qg_ref, f32[1,128]{1,0:T(1,128)} %bitcast.8), custom_call_target="tpu_custom_call" | custom-call | tf_op jit(solution)/shard_map/project/pallas_call | solution.py:46
  224.0 5.9 %collective-permute-start = (bf16[1536,768]{1,0:T(8,128)(2,1)}, bf16[1536,768]{1,0:T(8,128)(2,1)}, u32[]{:S(2)}, u32[]{:S(2)}) collective-permute-start(bf16[1536,768]{1,0:T(8,128)(2,1)} %get-tuple-element.8.b_ref), channel_id=1, source_target_pairs={{0,16},{16,32},{32,48},{48,64},{64,80},{80,96},{96,112},{1,17},{17... | collective-permute-start | bytes 7077896 | tf_op jit(solution)/shard_map/ppermute | solution.py:173
  229.9 1.3 collective-permute-start.1
  231.2 0.0 copy-done.5
  231.2 0.7 reshape.21.pat_ref
  231.9 97.4 %collective-permute-done.a_ref = bf16[1536,768]{1,0:T(8,128)(2,1)} collective-permute-done((bf16[1536,768]{1,0:T(8,128)(2,1)}, bf16[1536,768]{1,0:T(8,128)(2,1)}, u32[]{:S(2)}, u32[]{:S(2)}) %collective-permute-start) | collective-permute-done | bytes 2359328 | tf_op jit(solution)/shard_map/ppermute | solution.py:173
  329.3 0.0 collective-permute-done.1.c_ref
  329.3 23.7 %attention.1 = bf16[1536,384]{1,0:T(8,128)(2,1)} custom-call(s32[48]{0:T(128)} %reshape.21.pat_ref, s32[8]{0:T(128)} %cnt_ref.1, s32[1]{0:T(128)} %bitcast.t_ref, bf16[1536,384]{1,0:T(8,128)(2,1)} %get-tuple-element.7.q_ref, bf16[1536,768]{1,0:T(8,128)(2,1)} %collective-permute-done.a_ref, bf16[1536,768]{1,0:T(8,128)(2,1)} %get-tuple-element.8.b_ref, ...), custom_call_target="tpu_custom_call" | custom-call | tf_op jit(solution)/shard_map/attention/pallas_call | solution.py:148
  353.0 0.0 copy-done
  353.0 9.0 %convolution_convert_fusion = bf16[1536,3072]{1,0:T(8,128)(2,1)} fusion(bf16[1536,384]{1,0:T(8,128)(2,1)} %attention.1, bf16[384,3072]{1,0:T(8,128)(2,1)S(1)} %copy-done), kind=kOutput, calls=%fused_computation | convolution fusion | flops 3628597248 | bytes 12976128 | tf_op jit(solution)/shard_map/dot_general | solution.py:177
  362.0 0.0 copy-start.4
  362.0 0.0 reduce-scatter.2.cloned.1.call-update
  362.0 202.2 %reduce-scatter.2.cloned.1.call-done = bf16[192,3072]{1,0:T(8,128)(2,1)} async-done(((bf16[1536,3072]{1,0:T(8,128)(2,1)}), bf16[192,3072]{1,0:T(8,128)(2,1)}) %reduce-scatter.2.cloned.1.call-update) | async-done | bytes 1179664 | tf_op jit(solution)/shard_map/reduce_scatter | solution.py:176
  564.2 0.0 copy-done.4
  564.2 2.7 fusion.6
  (3 shorter events, 0.0 us)
Async XLA Ops:
  6.5 346.4 %copy-start = (bf16[384,3072]{1,0:T(8,128)(2,1)S(1)}, bf16[384,3072]{1,0:T(8,128)(2,1)}, u32[]{:S(2)}) copy-start(bf16[384,3072]{1,0:T(8,128)(2,1)} %param.17) | copy-start | bytes 7077892
  6.5 3.5 copy-start.1
  6.5 3.5 copy-start.2
  6.5 196.5 %all-gather.2.cloned.1.call-start = ((), (), s32[]{:S(2)}) async-start(), calls=%async_computation.1 | async-start | bytes 10616832 | tf_op jit(solution)/shard_map/all_gather | solution.py:168
  6.5 3.4 copy-start.3
  8.2 3.4 copy-start.6
  11.6 552.6 %reduce-scatter.2.cloned.1.call-start = ((), (), s32[]{:S(2)}) async-start(), calls=%async_computation.2 | async-start | bytes 10616832 | tf_op jit(solution)/shard_map/reduce_scatter | solution.py:176
  203.0 28.2 %copy-start.5 = (s32[3,4,4]{2,1,0:T(4,128)S(1)}, s32[3,4,4]{2,1,0:T(4,128)}, u32[]{:S(2)}) copy-start(s32[3,4,4]{2,1,0:T(4,128)} %param.18) | copy-start | bytes 580
  224.0 105.3 %collective-permute-start = (bf16[1536,768]{1,0:T(8,128)(2,1)}, bf16[1536,768]{1,0:T(8,128)(2,1)}, u32[]{:S(2)}, u32[]{:S(2)}) collective-permute-start(bf16[1536,768]{1,0:T(8,128)(2,1)} %get-tuple-element.8.b_ref), channel_id=1, source_target_pairs={{0,16},{16,32},{32,48},{48,64},{64,80},{80,96},{96,112},{1,17},{17... | collective-permute-start | bytes 7077896 | tf_op jit(solution)/shard_map/ppermute | solution.py:173
  229.9 99.4 %collective-permute-start.1 = (bf16[1536,768]{1,0:T(8,128)(2,1)}, bf16[1536,768]{1,0:T(8,128)(2,1)}, u32[]{:S(2)}, u32[]{:S(2)}) collective-permute-start(bf16[1536,768]{1,0:T(8,128)(2,1)} %get-tuple-element.8.b_ref), channel_id=1, source_target_pairs={{16,0},{32,16},{48,32},{64,48},{80,64},{96,80},{112,96},{17,1},{33... | collective-permute-start | bytes 7077896 | tf_op jit(solution)/shard_map/ppermute | solution.py:174
  362.0 202.2 %copy-start.4 = (f32[3072]{0:T(1024)S(1)}, f32[3072]{0:T(1024)}, u32[]{:S(2)}) copy-start(f32[3072]{0:T(1024)} %param.13) | copy-start | bytes 36868
Sparse Core Ops, SparseCore 0:
  11.7 191.2 all-gather.1
  362.1 202.0 reduce-scatter.1

commit v2 on v1

--- a/solution.py
+++ b/solution.py
@@ -16,64 +16,264 @@
 QSCALE = HD**-0.5 * 1.4426950408889634
 
 
-def modulate(rows, shift, mod_scale):
-    values = rows.astype(jnp.float32)
-    center = jnp.mean(values, axis=-1, keepdims=True)
-    centred = values - center
-    spread = jnp.mean(centred * centred, axis=-1, keepdims=True)
-    return (centred * lax.rsqrt(spread + 1e-06) * (1.0 + mod_scale) + shift).astype(jnp.bfloat16)
-
-
 def head_norm(values, gain):
     square = jnp.mean(values * values, axis=-1, keepdims=True)
     return (values * lax.rsqrt(square + 1e-06) * gain).astype(jnp.bfloat16)
 
 
-def project_kernel(x_ref, w_ref, qg_ref, kg_ref, q_ref, kv_ref):
-    x = x_ref[...]
-    heads = w_ref.shape[0]
-    for h in range(heads):
-        mixed = jnp.dot(x, w_ref[h], preferred_element_type=jnp.float32)
-        q_ref[:, h * HD : (h + 1) * HD] = head_norm(mixed[:, :HD], qg_ref[...])
-        kv_ref[:, h * HD : (h + 1) * HD] = head_norm(mixed[:, HD : 2 * HD], kg_ref[...])
-        kv_ref[:, (heads + h) * HD : (heads + h + 1) * HD] = mixed[:, 2 * HD :].astype(jnp.bfloat16)
-
-
-def project(normed, w, q_gain, k_gain):
-    heads, depth, width = w.shape
-    rows = normed.shape[0]
-    step = 192
+MESH = pl.DeviceIdType.MESH
+CHUNKS = 4
+SWAP, YP_OWN, YM_OWN, Z_OWN, YP_FWD, YM_FWD, YP_PEER, YM_PEER, Z_OPP = range(0, 4 * 9, 4)
+MESSAGES = 36
+SLICES = 8
+
+
+def place():
+    f, h, c = lax.axis_index("frame"), lax.axis_index("head"), lax.axis_index("rep")
+    return f // 2, f % 2, h // 2, h % 2, c
+
+
+def gather_kernel(heads, tok_ref, scale_ref, shift_ref, w_hbm, qg_ref, kg_ref, q_out, kv_out,
+                  xbuf, mine, w, qbuf, kvbuf, send, recv, halo_send, halo_recv, out_sem, w_sem):
+    x, zh, y, zl, c = place()
+    nx = lax.axis_size("frame") // 2
+    rows = mine.shape[0]
+    part = rows // CHUNKS
+    pos = y * 2 + zl
+    flip = (zh + c) % 2
+    yp, ym = {"head": (y + 1) % 4 * 2 + zl}, {"head": (y + 3) % 4 * 2 + zl}
+    zp = {"head": y * 2 + 1 - zl}
+    partner = {"frame": x * 2 + 1 - zh, "head": y * 2 + 1 - zl, "rep": 1 - c}
+    sibling = {"rep": 1 - c}
+    xn = {"frame": (x + nx + 2 * c - 1) % nx * 2 + zh, "rep": 1 - c}
+
+    barrier = pltpu.get_barrier_semaphore()
+    neighbours = (yp, ym, zp, partner, sibling, xn)
+    for device in neighbours:
+        pl.semaphore_signal(barrier, inc=1, device_id=device, device_id_type=MESH)
+
+    w_copy = pltpu.make_async_copy(w_hbm, w, w_sem)
+    w_copy.start()
+
+    def chunk(k):
+        return pl.ds(k * part, part)
+
+    for k in range(CHUNKS):
+        values = tok_ref[chunk(k), :].astype(jnp.float32)
+        center = jnp.mean(values, axis=-1, keepdims=True)
+        centred = values - center
+        spread = jnp.mean(centred * centred, axis=-1, keepdims=True)
+        normed = (centred * lax.rsqrt(spread + 1e-06) * scale_ref[...] + shift_ref[...]).astype(jnp.bfloat16)
+        mine[chunk(k), :] = normed
+
+        @pl.when(flip == 0)
+        def _():
+            xbuf[pos, chunk(k), :] = normed
+
+    pl.semaphore_wait(barrier, len(neighbours))
+
+    def slot_of(dy, dz):
+        return (y + dy) % 4 * 2 + (zl + dz) % 2
+
+    def message(number, k, slot, device):
+        there = xbuf.at[slot, chunk(k)]
+        return pltpu.make_async_remote_copy(
+            src_ref=there, dst_ref=there, send_sem=send.at[number + k], recv_sem=recv.at[number + k],
+            device_id=device, device_id_type=MESH,
+        )
+
+    def swap(k, slot):
+        return pltpu.make_async_remote_copy(
+            src_ref=mine.at[chunk(k)], dst_ref=xbuf.at[slot, chunk(k)], send_sem=send.at[SWAP + k],
+            recv_sem=recv.at[SWAP + k], device_id=partner, device_id_type=MESH,
+        )
+
+    @pl.when(flip == 1)
+    def _():
+        for k in (0, 3, 1, 2):
+            swap(k, y * 2 + 1 - zl).start()
+
+    def arrive(number, k, slot):
+        message(number, k, slot, zp).wait_recv()
+
+    def own(number, ks, device):
+        for k in ks:
+            message(number, k, pos, device).start()
+
+    for k, to_yp, to_ym in ((0, (0,), ()), (3, (), (3,)), (1, (1,), ()), (2, (), (2,))):
+        @pl.when(flip == 1)
+        def _():
+            swap(k, pos).wait_recv()
+
+        own(Z_OWN, (k,), zp)
+        own(YP_OWN, to_yp, yp)
+        own(YM_OWN, to_ym, ym)
+    own(YP_OWN, (2, 3), yp)
+    own(YM_OWN, (1, 0), ym)
+
+    below, above, across, facing = slot_of(3, 0), slot_of(1, 0), slot_of(0, 1), slot_of(2, 0)
+
+    def peer(k):
+        arrive(Z_OWN, k, across)
+        message(YP_PEER, k, across, yp).start()
+        message(YM_PEER, k, across, ym).start()
+
+    def forward_up(k):
+        arrive(YP_OWN, k, below)
+        message(YP_FWD, k, below, yp).start()
+
+    def forward_down(k):
+        arrive(YM_OWN, k, above)
+        message(YM_FWD, k, above, ym).start()
+
+    def opposite(number, k):
+        arrive(number, k, facing)
+        message(Z_OPP, k, facing, zp).start()
+
+    def second():
+        forward_up(0)
+        forward_down(3)
+        peer(0)
+        peer(3)
+        forward_up(1)
+        forward_down(2)
+        peer(1)
+        peer(2)
+        arrive(YP_OWN, 2, below)
+        arrive(YP_OWN, 3, below)
+
+    def third():
+        arrive(YM_OWN, 1, above)
+        arrive(YM_OWN, 0, above)
+
+    def fifth():
+        opposite(YP_FWD, 0)
+        opposite(YM_FWD, 3)
+        opposite(YP_FWD, 1)
+        opposite(YM_FWD, 2)
+
+    def sixth():
+        for k in range(CHUNKS):
+            arrive(YP_PEER, k, slot_of(3, 1))
+
+    def seventh():
+        for k in range(CHUNKS):
+            arrive(YM_PEER, k, slot_of(1, 1))
+
+    def eighth():
+        for k in range(CHUNKS):
+            arrive(Z_OPP, k, slot_of(2, 1))
+
+    order = (
+        (0, 0, None), (3, 0, second), (1, 0, third), (0, 1, None),
+        (2, 0, fifth), (3, 1, sixth), (1, 1, seventh), (2, 1, eighth),
+    )
+
+    def slice_rows(s):
+        return pl.ds(pl.multiple_of(s * rows, rows), rows)
+
+    def halo(s, slot, number, device):
+        return pltpu.make_async_remote_copy(
+            src_ref=kvbuf.at[slice_rows(s)], dst_ref=kv_out.at[slot, slice_rows(s)],
+            send_sem=halo_send.at[number + s], recv_sem=halo_recv.at[number + s],
+            device_id=device, device_id_type=MESH,
+        )
+
+    def out_copies(s):
+        return (
+            pltpu.make_async_copy(qbuf.at[slice_rows(s)], q_out.at[slice_rows(s)], out_sem.at[s]),
+            pltpu.make_async_copy(kvbuf.at[slice_rows(s)], kv_out.at[0, slice_rows(s)], out_sem.at[SLICES + s]),
+        )
+
+    def step(n, carry):
+        dy, dz = jnp.int32(0), jnp.int32(0)
+        for k, (one, two, handler) in enumerate(order):
+            dy = jnp.where(n == k, one, dy)
+            dz = jnp.where(n == k, two, dz)
+            if handler is not None:
+                pl.when(n == k)(handler)
+        slot = slot_of(dy, dz)
+        s = (y + dy) % 4 * 2 + (zl + dz + flip) % 2
+        here = slice_rows(s)
+
+        def head(h, carry):
+            mixed = jnp.dot(xbuf[slot], w[h], preferred_element_type=jnp.float32)
+            cols = pl.ds(pl.multiple_of(h * HD, HD), HD)
+            values = pl.ds(pl.multiple_of((heads + h) * HD, HD), HD)
+            qbuf[here, cols] = head_norm(mixed[:, :HD], qg_ref[...])
+            kvbuf[here, cols] = head_norm(mixed[:, HD : 2 * HD], kg_ref[...])
+            kvbuf[here, values] = mixed[:, 2 * HD :].astype(jnp.bfloat16)
+            return carry
+
+        lax.fori_loop(0, heads, head, 0)
+        halo(s, 2, SLICES, xn).start()
+        halo(s, 1, 0, sibling).start()
+        for copy in out_copies(s):
+            copy.start()
+        return carry
+
+    w_copy.wait()
+    lax.fori_loop(0, SLICES, step, 0)
+
+    @pl.when(flip == 1)
+    def _():
+        for k in range(CHUNKS):
+            swap(k, y * 2 + 1 - zl).wait_send()
+
+    for number, ks in ((YP_OWN, range(4)), (YM_OWN, range(4)), (Z_OWN, range(4)), (YP_FWD, (0, 1)), (YM_FWD, (2, 3)),
+                       (YP_PEER, range(4)), (YM_PEER, range(4)), (Z_OPP, range(4))):
+        for k in ks:
+            message(number, k, pos, zp).wait_send()
+
+    def finish(s, carry):
+        for copy in out_copies(s):
+            copy.wait()
+        halo(s, 1, 0, sibling).wait()
+        halo(s, 2, SLICES, xn).wait()
+        return carry
+
+    lax.fori_loop(0, SLICES, finish, 0)
+
+
+def gather_project(tokens, shift, mod_scale, w, q_gain, k_gain):
+    rows, depth = tokens.shape
+    heads = w.shape[0]
+    width = heads * HD
+    vmem = pl.BlockSpec(memory_space=pltpu.VMEM)
+    hbm = pl.BlockSpec(memory_space=pl.ANY)
+    dma = pltpu.SemaphoreType.DMA
     return pl.pallas_call(
-        project_kernel,
-        name="project",
-        grid=(rows // step,),
+        functools.partial(gather_kernel, heads),
+        name="gather_project",
         out_shape=(
-            jax.ShapeDtypeStruct((rows, heads * HD), jnp.bfloat16),
-            jax.ShapeDtypeStruct((rows, 2 * heads * HD), jnp.bfloat16),
+            jax.ShapeDtypeStruct((SLICES * rows, width), jnp.bfloat16),
+            jax.ShapeDtypeStruct((3, SLICES * rows, 2 * width), jnp.bfloat16),
         ),
-        in_specs=[
-            pl.BlockSpec((step, depth), lambda i: (i, 0)),
-            pl.BlockSpec((heads, depth, width), lambda i: (0, 0, 0), pipeline_mode=pl.Buffered(1)),
-            pl.BlockSpec((1, HD), lambda i: (0, 0)),
-            pl.BlockSpec((1, HD), lambda i: (0, 0)),
+        in_specs=[vmem, vmem, vmem, hbm, vmem, vmem],
+        out_specs=(hbm, hbm),
+        scratch_shapes=[
+            pltpu.VMEM((SLICES, rows, depth), jnp.bfloat16),
+            pltpu.VMEM((rows, depth), jnp.bfloat16),
+            pltpu.VMEM(w.shape, jnp.bfloat16),
+            pltpu.VMEM((SLICES * rows, width), jnp.bfloat16),
+            pltpu.VMEM((SLICES * rows, 2 * width), jnp.bfloat16),
+            dma((MESSAGES,)), dma((MESSAGES,)), dma((2 * SLICES,)), dma((2 * SLICES,)), dma((2 * SLICES,)), dma(()),
         ],
-        out_specs=(
-            pl.BlockSpec((step, heads * HD), lambda i: (i, 0)),
-            pl.BlockSpec((step, 2 * heads * HD), lambda i: (i, 0)),
+        compiler_params=pltpu.CompilerParams(
+            vmem_limit_bytes=VMEM_LIMIT, collective_id=0, has_side_effects=True
         ),
-        compiler_params=pltpu.CompilerParams(vmem_limit_bytes=VMEM_LIMIT),
-    )(normed, w, (q_gain * QSCALE)[None], k_gain[None])
-
-
-def attention_kernel(heads, pat_ref, cnt_ref, t_ref, q_ref, a_ref, b_ref, c_ref, out_ref, kwin, vwin, vext, acc, todo, sem):
+    )(tokens, (1.0 + mod_scale)[None], shift[None], w, (q_gain * QSCALE)[None], k_gain[None])
+
+
+def attention_kernel(heads, pat_ref, cnt_ref, t_ref, q_ref, kv_ref, out_ref, kwin, vwin, vext, acc, todo, sem):
     t = t_ref[0]
     width = heads * HD
-    windows = (a_ref, b_ref, c_ref)
+    slots = (2 - t % 2, 0, 1 + t % 2)
     copies = []
     for o in range(3):
         for part, into in ((0, kwin), (1, vwin)):
             copy = pltpu.make_async_copy(
-                windows[o].at[:, part * width : (part + 1) * width], into.at[o], sem.at[2 * o + part]
+                kv_ref.at[slots[o], :, part * width : (part + 1) * width], into.at[o], sem.at[2 * o + part]
             )
             copy.start()
             copies.append(copy)
@@ -139,7 +339,7 @@
     lax.fori_loop(0, GS, tile, 0)
 
 
-def attention(q, before, own, after, pattern, counts, t):
+def attention(q, kv, pattern, counts, t):
     rows, width = q.shape
     heads = width // HD
     smem = pl.BlockSpec(memory_space=pltpu.SMEM)
@@ -149,7 +349,7 @@
         functools.partial(attention_kernel, heads),
         name="attention",
         out_shape=jax.ShapeDtypeStruct((rows, width), jnp.bfloat16),
-        in_specs=[smem, smem, smem, vmem, hbm, hbm, hbm],
+        in_specs=[smem, smem, smem, vmem, hbm],
         out_specs=vmem,
         scratch_shapes=[
             pltpu.VMEM((3, rows, width), jnp.bfloat16),
@@ -160,25 +360,22 @@
             pltpu.SemaphoreType.DMA((6,)),
         ],
         compiler_params=pltpu.CompilerParams(vmem_limit_bytes=VMEM_LIMIT),
-    )(pattern.reshape(-1), counts, t.reshape(1), q, before, own, after)
+    )(pattern.reshape(-1), counts, t.reshape(1), q, kv)
 
 
 def per_device(tokens, shift, mod_scale, gate, w_qkv, q_gain, k_gain, w_out, pattern, counts):
-    normed = modulate(tokens, shift, mod_scale)
-    gathered = lax.all_gather(normed, "head", axis=0, tiled=True)
-    q, kv = project(gathered, jnp.transpose(w_qkv, (1, 0, 2)), q_gain, k_gain)
-    size = lax.axis_size("frame")
-    up = [(i, (i + 1) % size) for i in range(size - 1)]
-    down = [(j, i) for i, j in up]
-    before = lax.ppermute(kv, "frame", up)
-    after = lax.ppermute(kv, "frame", down)
-    attn = attention(q, before, kv, after, pattern, counts, lax.axis_index("frame"))
+    q, kv = gather_project(tokens, shift, mod_scale, jnp.transpose(w_qkv, (1, 0, 2)), q_gain, k_gain)
+    block = lax.axis_index("frame") // 2 * 2 + lax.axis_index("rep")
+    attn = attention(q, kv, pattern, counts, block)
     result = lax.psum_scatter(
         jnp.dot(attn, w_out, preferred_element_type=jnp.float32).astype(jnp.bfloat16),
         "head",
         scatter_dimension=0,
         tiled=True,
-    ).astype(jnp.float32)
+    )
+    size = lax.axis_size("frame")
+    swap = [(f * 2 + c, (f // 2 * 2 + c) * 2 + f % 2) for f in range(size) for c in range(2)]
+    result = lax.ppermute(result, ("frame", "rep"), swap).astype(jnp.float32)
     return (tokens.astype(jnp.float32) + gate * result).astype(jnp.bfloat16)
 
 

time: 574 us -> 350 us (0.61)
  waiting for transfers between devices: 490 us -> 202 us
  Pallas kernels: 44.7 us -> 115 us
    all_gather x1 -> x0, waiting for transfers between devices: 191 us -> none  [per_device(): gathered = lax.all_gather(normed, 'head', axis=0, tiled=True)]
    ppermute x2 -> x1, waiting for transfers between devices: 97.4 us -> 14.3 us  [per_device(): result = lax.ppermute(result, ('frame', 'rep'), swap).astype(jnp.float32)]
    pallas_call x1, Pallas kernels: 21 us -> 87.4 us  [gather_project(): pl.pallas_call(functools.partial(gather_kernel, heads), name='gather_proj...]
    reduce_scatter x1, waiting for transfers between devices: 202 us -> 188 us  [per_device(): lax.psum_scatter(jnp.dot(attn, w_out, preferred_element_type=jnp.float32)...]
  transfers between devices with their start and end apart: 4 -> 2, of which waited for: 3 -> 2; matrix products, arithmetic and copies ran while one was open for 0% -> 0% of each run, Pallas kernels for 0% -> 0%
where the time goes in v2:
time: 350 us
  waiting for transfers between devices  202 us (58%)
  Pallas kernels  115 us (33%)
  between operations  13.4 us (4%)
  matrix products  8.84 us (3%)
  starting transfers between devices  4.97 us (1%)
  other arithmetic  4.03 us (1%)
    reduce_scatter x1, waiting for transfers between devices, per_device(): lax.psum_scatter(jnp.dot(attn, w_out, preferred_element_type=jnp.float32)...  188 us
    pallas_call x1, Pallas kernels, gather_project(): pl.pallas_call(functools.partial(gather_kernel, heads), name='gather_proj...  87.4 us
    pallas_call x1, Pallas kernels, attention(): pl.pallas_call(functools.partial(attention_kernel, heads), name='attentio...  28 us
    ppermute x1, waiting for transfers between devices, per_device(): result = lax.ppermute(result, ('frame', 'rep'), swap).astype(jnp.float32)  14.3 us
    dot_general x1, matrix products, per_device(): jnp.dot(attn, w_out, preferred_element_type=jnp.float32)  8.84 us
  transfers between devices with their start and end apart: 2, of which 2 were waited for; matrix products, arithmetic and copies ran while one was open for 0% of the time, Pallas kernels for 0%

profile of v2, /device:TPU:1, one launch (start us, length us, event | category | flops | bytes accessed | tf_op | source)
XLA Modules:
  0.0 349.9 jit_solution(5645573790699308930)
XLA Ops:
  6.5 0.0 copy-start
  6.5 0.0 reduce-scatter.2.cloned.1.call-start
  6.5 1.3 multiply_bitcast_fusion.qg_ref
  7.8 1.4 reshape.7.pat_ref
  9.2 1.3 broadcast_add_fusion
  10.5 87.4 %gather_project.1 = (bf16[1536,384]{1,0:T(8,128)(2,1)}, bf16[3,1536,768]{2,1,0:T(8,128)(2,1)}) custom-call(bf16[192,3072]{1,0:T(8,128)(2,1)} %tok_ref.1, f32[1,3072]{1,0:T(1,128)} %bitcast.10, f32[1,3072]{1,0:T(1,128)} %bitcast.11, bf16[3,3072,384]{2,1,0:T(8,128)(2,1)} %bitcast.9, f32[1,128]{1,0:T(1,128)} %multiply_bitcast_fusion.qg_ref, f32[1,128]{1,0:T(1,128)} %bitcast.12), custom_call_target="tpu_custom_call" | custom-call | tf_op jit(solution)/shard_map/gather_project/pallas_call | solution.py:245
  98.0 28.0 %attention.1 = bf16[1536,384]{1,0:T(8,128)(2,1)} custom-call(s32[48]{0:T(128)} %reshape.7.pat_ref, s32[8]{0:T(128)} %cnt_ref.1, s32[1]{0:T(128)} %bitcast.t_ref, bf16[1536,384]{1,0:T(8,128)(2,1)} %get-tuple-element.7.q_ref, bf16[3,1536,768]{2,1,0:T(8,128)(2,1)} %get-tuple-element.8.kv_ref), custom_call_target="tpu_custom_call" | custom-call | tf_op jit(solution)/shard_map/attention/pallas_call | solution.py:348
  125.9 0.0 copy-done
  125.9 8.8 %convolution_convert_fusion = bf16[1536,3072]{1,0:T(8,128)(2,1)} fusion(bf16[1536,384]{1,0:T(8,128)(2,1)} %attention.1, bf16[384,3072]{1,0:T(8,128)(2,1)S(1)} %copy-done), kind=kOutput, calls=%fused_computation | convolution fusion | flops 3628597248 | bytes 12976128 | tf_op jit(solution)/shard_map/dot_general | solution.py:371
  134.8 0.0 copy-start.1
  134.8 0.0 copy-start.2
  134.8 0.0 reduce-scatter.2.cloned.1.call-update
  134.8 187.6 %reduce-scatter.2.cloned.1.call-done = bf16[192,3072]{1,0:T(8,128)(2,1)} async-done(((bf16[1536,3072]{1,0:T(8,128)(2,1)}), bf16[192,3072]{1,0:T(8,128)(2,1)}) %reduce-scatter.2.cloned.1.call-update) | async-done | bytes 1179664 | tf_op jit(solution)/shard_map/reduce_scatter | solution.py:370
  322.4 5.0 %collective-permute-start = (bf16[192,3072]{1,0:T(8,128)(2,1)}, bf16[192,3072]{1,0:T(8,128)(2,1)S(1)}, u32[]{:S(2)}, u32[]{:S(2)}) collective-permute-start(bf16[192,3072]{1,0:T(8,128)(2,1)} %reduce-scatter.2.cloned.1.call-done), channel_id=1, source_target_pairs={{0,0},{1,16},{16,1},{17,17},{32,32},{33,48},{48,33},{49,49},{64,64... | collective-permute-start | bytes 3538952 | tf_op jit(solution)/shard_map/ppermute | solution.py:378
  327.3 14.3 %collective-permute-done = bf16[192,3072]{1,0:T(8,128)(2,1)S(1)} collective-permute-done((bf16[192,3072]{1,0:T(8,128)(2,1)}, bf16[192,3072]{1,0:T(8,128)(2,1)S(1)}, u32[]{:S(2)}, u32[]{:S(2)}) %collective-permute-start) | collective-permute-done | bytes 1179680 | tf_op jit(solution)/shard_map/ppermute | solution.py:378
  341.6 0.0 copy-done.1
  341.6 0.0 copy-done.2
  341.6 1.4 add_convert_fusion
Async XLA Ops:
  6.5 119.4 %copy-start = (bf16[384,3072]{1,0:T(8,128)(2,1)S(1)}, bf16[384,3072]{1,0:T(8,128)(2,1)}, u32[]{:S(2)}) copy-start(bf16[384,3072]{1,0:T(8,128)(2,1)} %param.17) | copy-start | bytes 7077892
  6.5 315.8 %reduce-scatter.2.cloned.1.call-start = ((), (), s32[]{:S(2)}) async-start(), calls=%async_computation.1 | async-start | bytes 10616832 | tf_op jit(solution)/shard_map/reduce_scatter | solution.py:370
  134.8 206.8 %copy-start.1 = (bf16[192,3072]{1,0:T(8,128)(2,1)S(1)}, bf16[192,3072]{1,0:T(8,128)(2,1)}, u32[]{:S(2)}) copy-start(bf16[192,3072]{1,0:T(8,128)(2,1)} %tok_ref.1) | copy-start | bytes 3538948
  134.8 206.8 %copy-start.2 = (f32[3072]{0:T(1024)S(1)}, f32[3072]{0:T(1024)}, u32[]{:S(2)}) copy-start(f32[3072]{0:T(1024)} %param.13) | copy-start | bytes 36868
  322.4 19.2 %collective-permute-start = (bf16[192,3072]{1,0:T(8,128)(2,1)}, bf16[192,3072]{1,0:T(8,128)(2,1)S(1)}, u32[]{:S(2)}, u32[]{:S(2)}) collective-permute-start(bf16[192,3072]{1,0:T(8,128)(2,1)} %reduce-scatter.2.cloned.1.call-done), channel_id=1, source_target_pairs={{0,0},{1,16},{16,1},{17,17},{32,32},{33,48},{48,33},{49,49},{64,64... | collective-permute-start | bytes 3538952 | tf_op jit(solution)/shard_map/ppermute | solution.py:378
Sparse Core Ops, SparseCore 0:
  134.9 187.3 reduce-scatter.1

commit v3 on v2

--- a/solution.py
+++ b/solution.py
@@ -25,6 +25,8 @@
 CHUNKS = 4
 SWAP, YP_OWN, YM_OWN, Z_OWN, YP_FWD, YM_FWD, YP_PEER, YM_PEER, Z_OPP = range(0, 4 * 9, 4)
 MESSAGES = 36
+W_YP, W_YM, W_YP_FWD, W_YM_FWD, W_ZF, W_ZF_ALL, W_XP, W_XM, W_SIB, W_SIB_ALL = 0, 1, 2, 3, 4, 7, 8, 14, 20, 38
+W_MESSAGES = 39
 SLICES = 8
 
 
@@ -33,8 +35,8 @@
     return f // 2, f % 2, h // 2, h % 2, c
 
 
-def gather_kernel(heads, tok_ref, scale_ref, shift_ref, w_hbm, qg_ref, kg_ref, q_out, kv_out,
-                  xbuf, mine, w, qbuf, kvbuf, send, recv, halo_send, halo_recv, out_sem, w_sem):
+def gather_kernel(heads, tok_ref, scale_ref, shift_ref, w_hbm, qg_ref, kg_ref, wo_ref, q_out, kv_out, wall,
+                  xbuf, mine, w, qbuf, kvbuf, send, recv, halo_send, halo_recv, out_sem, w_sem, wo_send, wo_recv):
     x, zh, y, zl, c = place()
     nx = lax.axis_size("frame") // 2
     rows = mine.shape[0]
@@ -47,8 +49,11 @@
     sibling = {"rep": 1 - c}
     xn = {"frame": (x + nx + 2 * c - 1) % nx * 2 + zh, "rep": 1 - c}
 
+    zf = {"frame": x * 2 + 1 - zh, "head": y * 2 + 1 - zl}
+    xp, xm = {"frame": (x + 1) % nx * 2 + zh}, {"frame": (x + nx - 1) % nx * 2 + zh}
+
     barrier = pltpu.get_barrier_semaphore()
-    neighbours = (yp, ym, zp, partner, sibling, xn)
+    neighbours = (yp, ym, zp, partner, sibling, xn, zf, xp, xm)
     for device in neighbours:
         pl.semaphore_signal(barrier, inc=1, device_id=device, device_id_type=MESH)
 
@@ -93,6 +98,80 @@
         for k in (0, 3, 1, 2):
             swap(k, y * 2 + 1 - zl).start()
 
+    half = wo_ref.shape[-1] // 2
+
+    def piece(number, src, dst, device):
+        return pltpu.make_async_remote_copy(
+            src_ref=src, dst_ref=dst, send_sem=wo_send.at[number], recv_sem=wo_recv.at[number],
+            device_id=device, device_id_type=MESH,
+        )
+
+    def held(dy, zl_, k):
+        return wall.at[dy, zl_, c, k]
+
+    def w_first(number, dy, device):
+        return piece(number, wo_ref.at[c, x], held(dy, zl, x), device)
+
+    def w_forward(number, dy, cols, device):
+        return piece(number, held(dy, zl, x).at[:, cols], held(2, zl, x).at[:, cols], device)
+
+    def w_diagonal(dy, zl_):
+        return piece(W_ZF + dy - 1, held(dy, zl_, x), held(dy, zl_, x), zf)
+
+    def w_diagonal_all(zl_):
+        return piece(W_ZF_ALL, wo_ref.at[c], wall.at[0, zl_, c], zf)
+
+    def w_along(number, dy, z, k, device):
+        return piece(number + 2 * (dy - 1) + z, held(dy, (zl + z) % 2, k), held(dy, (zl + z) % 2, k), device)
+
+    def w_sibling(which, dy, z, core):
+        there = wall.at[dy, (zl + z) % 2, core, (x + which) % 4]
+        return piece(W_SIB + 6 * {0: 0, 1: 1, 3: 2}[which] + 2 * (dy - 1) + z, there, there, sibling)
+
+    def w_sibling_all(core):
+        there = wall.at[0, 1 - zl, core]
+        return piece(W_SIB_ALL, there, there, sibling)
+
+    def w_spread(dy, z):
+        w_along(W_XP, dy, z, x, xp).start()
+        w_along(W_XM, dy, z, x, xm).start()
+        w_sibling(0, dy, z, c).start()
+
+    low, high = pl.ds(0, half), pl.ds(half, half)
+    w_first(W_YP, 3, yp).start()
+    w_first(W_YM, 1, ym).start()
+
+    def w_one():
+        w_first(W_YP, 3, yp).wait_recv()
+        w_forward(W_YP_FWD, 3, low, yp).start()
+        w_diagonal(3, zl).start()
+        w_spread(3, 0)
+        w_first(W_YM, 1, ym).wait_recv()
+        w_forward(W_YM_FWD, 1, high, ym).start()
+        w_diagonal(1, zl).start()
+        w_spread(1, 0)
+
+    def w_two():
+        w_forward(W_YP_FWD, 2, low, yp).wait_recv()
+        w_forward(W_YM_FWD, 2, high, ym).wait_recv()
+        w_diagonal(2, zl).start()
+        w_spread(2, 0)
+        w_diagonal_all(zl).start()
+        for dy in (3, 1):
+            w_diagonal(dy, 1 - zl).wait_recv()
+            w_spread(dy, 1)
+
+    def w_three():
+        w_diagonal(2, 1 - zl).wait_recv()
+        w_spread(2, 1)
+
+    def w_four(z):
+        for dy in (3, 1, 2):
+            w_along(W_XP, dy, z, (x + 3) % 4, xp).wait_recv()
+            w_sibling(3, dy, z, c).start()
+            w_along(W_XM, dy, z, (x + 1) % 4, xm).wait_recv()
+            w_sibling(1, dy, z, c).start()
+
     def arrive(number, k, slot):
         message(number, k, slot, zp).wait_recv()
 
@@ -131,6 +210,7 @@
         message(Z_OPP, k, facing, zp).start()
 
     def second():
+        w_one()
         forward_up(0)
         forward_down(3)
         peer(0)
@@ -143,6 +223,7 @@
         arrive(YP_OWN, 3, below)
 
     def third():
+        w_two()
         arrive(YM_OWN, 1, above)
         arrive(YM_OWN, 0, above)
 
@@ -151,6 +232,7 @@
         opposite(YM_FWD, 3)
         opposite(YP_FWD, 1)
         opposite(YM_FWD, 2)
+        w_three()
 
     def sixth():
         for k in range(CHUNKS):
@@ -214,6 +296,10 @@
 
     w_copy.wait()
     lax.fori_loop(0, SLICES, step, 0)
+    w_diagonal_all(1 - zl).wait_recv()
+    w_sibling_all(c).start()
+    w_four(0)
+    w_four(1)
 
     @pl.when(flip == 1)
     def _():
@@ -233,9 +319,22 @@
         return carry
 
     lax.fori_loop(0, SLICES, finish, 0)
-
-
-def gather_project(tokens, shift, mod_scale, w, q_gain, k_gain):
+    w_first(W_YP, 3, yp).wait_send()
+    w_first(W_YM, 1, ym).wait_send()
+    w_forward(W_YP_FWD, 2, low, yp).wait_send()
+    w_forward(W_YM_FWD, 2, high, ym).wait_send()
+    w_diagonal_all(zl).wait_send()
+    w_sibling_all(1 - c).wait()
+    for dy in (1, 2, 3):
+        w_diagonal(dy, zl).wait_send()
+        for z in (0, 1):
+            w_along(W_XP, dy, z, x, xp).wait_send()
+            w_along(W_XM, dy, z, x, xm).wait_send()
+            for which in (0, 1, 3):
+                w_sibling(which, dy, z, 1 - c).wait()
+
+
+def gather_project(tokens, shift, mod_scale, w, q_gain, k_gain, w_out):
     rows, depth = tokens.shape
     heads = w.shape[0]
     width = heads * HD
@@ -248,9 +347,10 @@
         out_shape=(
             jax.ShapeDtypeStruct((SLICES * rows, width), jnp.bfloat16),
             jax.ShapeDtypeStruct((3, SLICES * rows, 2 * width), jnp.bfloat16),
+            jax.ShapeDtypeStruct((4, 2) + w_out.shape, jnp.bfloat16),
         ),
-        in_specs=[vmem, vmem, vmem, hbm, vmem, vmem],
-        out_specs=(hbm, hbm),
+        in_specs=[vmem, vmem, vmem, hbm, vmem, vmem, hbm],
+        out_specs=(hbm, hbm, hbm),
         scratch_shapes=[
             pltpu.VMEM((SLICES, rows, depth), jnp.bfloat16),
             pltpu.VMEM((rows, depth), jnp.bfloat16),
@@ -258,11 +358,12 @@
             pltpu.VMEM((SLICES * rows, width), jnp.bfloat16),
             pltpu.VMEM((SLICES * rows, 2 * width), jnp.bfloat16),
             dma((MESSAGES,)), dma((MESSAGES,)), dma((2 * SLICES,)), dma((2 * SLICES,)), dma((2 * SLICES,)), dma(()),
+            dma((W_MESSAGES,)), dma((W_MESSAGES,)),
         ],
         compiler_params=pltpu.CompilerParams(
             vmem_limit_bytes=VMEM_LIMIT, collective_id=0, has_side_effects=True
         ),
-    )(tokens, (1.0 + mod_scale)[None], shift[None], w, (q_gain * QSCALE)[None], k_gain[None])
+    )(tokens, (1.0 + mod_scale)[None], shift[None], w, (q_gain * QSCALE)[None], k_gain[None], w_out)
 
 
 def attention_kernel(heads, pat_ref, cnt_ref, t_ref, q_ref, kv_ref, out_ref, kwin, vwin, vext, acc, todo, sem):
@@ -363,20 +464,174 @@
     )(pattern.reshape(-1), counts, t.reshape(1), q, kv)
 
 
+def finish_kernel(attn, tok_ref, gate_ref, wo_ref, wall, out_ref, rows_in, wv, acc, a_send, a_recv, x_send, x_recv, s_send, s_recv, w_sem, own_sem):
+    x, zh, y, zl, c = place()
+    nx = lax.axis_size("frame") // 2
+    rows = tok_ref.shape[0]
+    depth = tok_ref.shape[1]
+    pos = y * 2 + zl
+    straight = zh == c
+    sibling = {"rep": 1 - c}
+    xp, xm = {"frame": (x + 1) % nx * 2 + zh}, {"frame": (x + nx - 1) % nx * 2 + zh}
+
+    def owner(s):
+        return {"frame": x * 2 + c, "head": s, "rep": zh}
+
+    def others(s):
+        return jnp.logical_or(s != pos, jnp.logical_not(straight))
+
+    barrier = pltpu.get_barrier_semaphore()
+    for device in (sibling, xp, xm):
+        pl.semaphore_signal(barrier, inc=1, device_id=device, device_id_type=MESH)
+
+    def greet(s, carry):
+        @pl.when(others(s))
+        def _():
+            pl.semaphore_signal(barrier, inc=1, device_id=owner(s), device_id_type=MESH)
+
+        return carry
+
+    lax.fori_loop(0, SLICES, greet, 0)
+
+    def load(dy, k):
+        return pltpu.make_async_copy(wall.at[dy, :, :, k], wv.at[dy, :, :, k], w_sem.at[4 * dy + k])
+
+    def loads(act):
+        act(pltpu.make_async_copy(wo_ref, wv.at[0, zl], w_sem.at[0]))
+        act(pltpu.make_async_copy(wall.at[0, 1 - zl], wv.at[0, 1 - zl], w_sem.at[1]))
+
+    loads(lambda copy: copy.start())
+    for dy in (1, 3, 2):
+        for which in (0, 1, 3):
+            load(dy, (x + which) % 4).start()
+    pl.semaphore_wait(barrier, jnp.where(straight, SLICES + 2, SLICES + 3))
+
+    def hand_out(s, source):
+        return pltpu.make_async_remote_copy(
+            src_ref=attn.at[pl.ds(pl.multiple_of(s * rows, rows), rows)], dst_ref=rows_in.at[source],
+            send_sem=a_send.at[s], recv_sem=a_recv.at[source], device_id=owner(s), device_id_type=MESH,
+        )
+
+    def keep():
+        return pltpu.make_async_copy(
+            attn.at[pl.ds(pl.multiple_of(pos * rows, rows), rows)], rows_in.at[pos], own_sem
+        )
+
+    def scatter(n, carry):
+        s = (pos + n) % SLICES
+
+        @pl.when(others(s))
+        def _():
+            hand_out(s, pos).start()
+
+        return carry
+
+    lax.fori_loop(0, SLICES, scatter, 0)
+
+    @pl.when(straight)
+    def _():
+        keep().start()
+
+    def far(number, dy, z, k, device):
+        return pltpu.make_async_remote_copy(
+            src_ref=wall.at[dy, z, c, k], dst_ref=wv.at[dy, z, c, k], send_sem=x_send.at[number + dy],
+            recv_sem=x_recv.at[number + dy], device_id=device, device_id_type=MESH,
+        )
+
+    def share(number, dy, z, core):
+        there = wv.at[dy, z, core, (x + 2) % 4]
+        return pltpu.make_async_remote_copy(
+            src_ref=there, dst_ref=there, send_sem=s_send.at[number + dy], recv_sem=s_recv.at[number + dy],
+            device_id=sibling, device_id_type=MESH,
+        )
+
+    for dy in (1, 3, 2):
+        far(0, dy, 0, (x + 3) % 4, xp).start()
+        far(4, dy, 1, (x + 1) % 4, xm).start()
+
+    acc[...] = tok_ref[...].astype(jnp.float32)
+    cols = min(512, depth)
+
+    def add(dy, z):
+        source = (y + dy) % 4 * 2 + (zl + z) % 2
+        kept = jnp.logical_and(straight, source == pos)
+
+        @pl.when(kept)
+        def _():
+            keep().wait()
+
+        @pl.when(jnp.logical_not(kept))
+        def _():
+            hand_out(0, source).wait_recv()
+
+        def column(n, carry):
+            here = pl.ds(pl.multiple_of(n * cols, cols), cols)
+            weight = wv[dy, (zl + z) % 2, :, :, :, here].reshape(rows_in.shape[2], cols)
+            acc[:, here] += gate_ref[:, here] * jnp.dot(rows_in[source], weight, preferred_element_type=jnp.float32)
+            return carry
+
+        lax.fori_loop(0, depth // cols, column, 0)
+
+    loads(lambda copy: copy.wait())
+    add(0, 0)
+    add(0, 1)
+    for dy in (1, 3, 2):
+        far(0, dy, 0, (x + 2) % 4, xp).wait_recv()
+        share(0, dy, 0, c).start()
+        far(4, dy, 1, (x + 2) % 4, xm).wait_recv()
+        share(4, dy, 1, c).start()
+        for which in (0, 1, 3):
+            load(dy, (x + which) % 4).wait()
+        share(0, dy, 0, 1 - c).wait_recv()
+        share(4, dy, 1, 1 - c).wait_recv()
+        add(dy, 0)
+        add(dy, 1)
+    out_ref[...] = acc[...].astype(jnp.bfloat16)
+
+    def sent(s, carry):
+        @pl.when(others(s))
+        def _():
+            hand_out(s, pos).wait_send()
+
+        return carry
+
+    lax.fori_loop(0, SLICES, sent, 0)
+    for dy in (1, 3, 2):
+        far(0, dy, 0, (x + 3) % 4, xp).wait_send()
+        far(4, dy, 1, (x + 1) % 4, xm).wait_send()
+        share(0, dy, 0, c).wait_send()
+        share(4, dy, 1, c).wait_send()
+
+
+def finish(attn, tokens, gate, w_out, wall):
+    rows, depth = tokens.shape
+    vmem = pl.BlockSpec(memory_space=pltpu.VMEM)
+    hbm = pl.BlockSpec(memory_space=pl.ANY)
+    dma = pltpu.SemaphoreType.DMA
+    return pl.pallas_call(
+        finish_kernel,
+        name="finish",
+        out_shape=jax.ShapeDtypeStruct((rows, depth), jnp.bfloat16),
+        in_specs=[hbm, vmem, vmem, hbm, hbm],
+        out_specs=vmem,
+        scratch_shapes=[
+            pltpu.VMEM((SLICES, rows, attn.shape[1]), jnp.bfloat16),
+            pltpu.VMEM(wall.shape, jnp.bfloat16),
+            pltpu.VMEM((rows, depth), jnp.float32),
+            dma((SLICES,)), dma((SLICES,)), dma((8,)), dma((8,)), dma((8,)), dma((8,)), dma((16,)), dma(()),
+        ],
+        compiler_params=pltpu.CompilerParams(
+            vmem_limit_bytes=VMEM_LIMIT, collective_id=1, has_side_effects=True
+        ),
+    )(attn, tokens, gate[None], w_out, wall)
+
+
 def per_device(tokens, shift, mod_scale, gate, w_qkv, q_gain, k_gain, w_out, pattern, counts):
-    q, kv = gather_project(tokens, shift, mod_scale, jnp.transpose(w_qkv, (1, 0, 2)), q_gain, k_gain)
+    w_parts = w_out.reshape(2, 4, w_out.shape[0] // 8, w_out.shape[1])
+    q, kv, wall = gather_project(tokens, shift, mod_scale, jnp.transpose(w_qkv, (1, 0, 2)), q_gain, k_gain, w_parts)
     block = lax.axis_index("frame") // 2 * 2 + lax.axis_index("rep")
     attn = attention(q, kv, pattern, counts, block)
-    result = lax.psum_scatter(
-        jnp.dot(attn, w_out, preferred_element_type=jnp.float32).astype(jnp.bfloat16),
-        "head",
-        scatter_dimension=0,
-        tiled=True,
-    )
-    size = lax.axis_size("frame")
-    swap = [(f * 2 + c, (f // 2 * 2 + c) * 2 + f % 2) for f in range(size) for c in range(2)]
-    result = lax.ppermute(result, ("frame", "rep"), swap).astype(jnp.float32)
-    return (tokens.astype(jnp.float32) + gate * result).astype(jnp.bfloat16)
+    return finish(attn, tokens, gate, w_parts, wall)
 
 
 def solution(mesh):

time: 350 us -> 179 us (0.51)
  the two profiles are of different devices: /device:TPU:1 before, /device:TPU:24 now
where the time goes in v3:
time: 179 us
  Pallas kernels  173 us (97%)
  local copies, waits for them, and re-layouts  3.66 us (2%)
  other arithmetic  2.45 us (1%)
    pallas_call x1, Pallas kernels, gather_project(): pl.pallas_call(functools.partial(gather_kernel, heads), name='gather_proj...  97.9 us
    pallas_call x1, Pallas kernels, finish(): pl.pallas_call(finish_kernel, name='finish', out_shape=jax.ShapeDtypeStru...  48.9 us
    pallas_call x1, Pallas kernels, attention(): pl.pallas_call(functools.partial(attention_kernel, heads), name='attentio...  26.2 us

profile of v3, /device:TPU:24, one launch (start us, length us, event | category | flops | bytes accessed | tf_op | source)
XLA Modules:
  0.0 179.2 jit_solution(16102358970442966577)
XLA Ops:
  0.0 1.1 multiply_bitcast_fusion.qg_ref
  1.1 1.3 reshape.9.pat_ref
  2.4 1.3 broadcast_add_fusion
  3.7 97.9 %gather_project.1 = (bf16[1536,384]{1,0:T(8,128)(2,1)}, bf16[3,1536,768]{2,1,0:T(8,128)(2,1)}, bf16[4,2,2,4,48,3072]{5,4,3,2,1,0:T(8,128)(2,1)}) custom-call(bf16[192,3072]{1,0:T(8,128)(2,1)} %tok_ref.3, f32[1,3072]{1,0:T(1,128)} %bitcast.12, f32[1,3072]{1,0:T(1,128)} %bitcast.13, bf16[3,3072,384]{2,1,0:T(8,128)(2,1)} %bitcast.11, ...), custom_call_target="tpu_custom_call" | custom-call | tf_op jit(solution)/shard_map/gather_project/pallas_call | solution.py:344
  101.6 26.2 %attention.1.attn = bf16[1536,384]{1,0:T(8,128)(2,1)} custom-call(s32[48]{0:T(128)} %reshape.9.pat_ref, s32[8]{0:T(128)} %cnt_ref.1, s32[1]{0:T(128)} %bitcast.t_ref, bf16[1536,384]{1,0:T(8,128)(2,1)} %get-tuple-element.8.q_ref, bf16[3,1536,768]{2,1,0:T(8,128)(2,1)} %get-tuple-element.9.kv_ref), custom_call_target="tpu_custom_call" | custom-call | tf_op jit(solution)/shard_map/attention/pallas_call | solution.py:449
  127.9 48.9 %finish.1 = bf16[192,3072]{1,0:T(8,128)(2,1)} custom-call(bf16[1536,384]{1,0:T(8,128)(2,1)} %attention.1.attn, bf16[192,3072]{1,0:T(8,128)(2,1)} %tok_ref.3, f32[1,3072]{1,0:T(1,128)} %bitcast.14, bf16[2,4,48,3072]{3,2,1,0:T(8,128)(2,1)} %bitcast.10, bf16[4,2,2,4,48,3072]{5,4,3,2,1,0:T(8,128)(2,1)} %get-tuple-element.10.wall), custom_call_target="tpu_custom_call" | custom-call | tf_op jit(solution)/shard_map/finish/pallas_call | solution.py:611
  176.8 2.4 %copy.12 = bf16[192,3072]{1,0:T(8,128)(2,1)} copy(bf16[192,3072]{1,0:T(8,128)(2,1)} %finish.1) | data formatting | bytes 2359296

commit v4 on v3

--- a/solution.py
+++ b/solution.py
@@ -12,6 +12,7 @@
 HD = 128
 NT = 8
 ROWS = GS * TILE
+NONE = 3 * GS
 VMEM_LIMIT = 56 * 1024 * 1024
 QSCALE = HD**-0.5 * 1.4426950408889634
 
@@ -24,9 +25,10 @@
 MESH = pl.DeviceIdType.MESH
 CHUNKS = 4
 SWAP, YP_OWN, YM_OWN, Z_OWN, YP_FWD, YM_FWD, YP_PEER, YM_PEER, Z_OPP = range(0, 4 * 9, 4)
+Z_BELOW, Z_ABOVE = YP_PEER, YM_PEER
 MESSAGES = 36
 W_YP, W_YM, W_YP_FWD, W_YM_FWD, W_ZF, W_ZF_ALL, W_XP, W_XM, W_SIB, W_SIB_ALL = 0, 1, 2, 3, 4, 7, 8, 14, 20, 38
-W_MESSAGES = 39
+W_MESSAGES = 40
 SLICES = 8
 
 
@@ -57,18 +59,22 @@
     for device in neighbours:
         pl.semaphore_signal(barrier, inc=1, device_id=device, device_id_type=MESH)
 
-    w_copy = pltpu.make_async_copy(w_hbm, w, w_sem)
-    w_copy.start()
+    w_copies = [
+        pltpu.make_async_copy(w_hbm.at[h], w.at[:, h * 3 * HD : (h + 1) * 3 * HD], w_sem.at[h]) for h in range(heads)
+    ]
+    for copy in w_copies:
+        copy.start()
 
     def chunk(k):
         return pl.ds(k * part, part)
 
+    scale = 1.0 + scale_ref[...]
     for k in range(CHUNKS):
         values = tok_ref[chunk(k), :].astype(jnp.float32)
         center = jnp.mean(values, axis=-1, keepdims=True)
         centred = values - center
         spread = jnp.mean(centred * centred, axis=-1, keepdims=True)
-        normed = (centred * lax.rsqrt(spread + 1e-06) * scale_ref[...] + shift_ref[...]).astype(jnp.bfloat16)
+        normed = (centred * lax.rsqrt(spread + 1e-06) * scale + shift_ref[...]).astype(jnp.bfloat16)
         mine[chunk(k), :] = normed
 
         @pl.when(flip == 0)
@@ -118,8 +124,9 @@
     def w_diagonal(dy, zl_):
         return piece(W_ZF + dy - 1, held(dy, zl_, x), held(dy, zl_, x), zf)
 
-    def w_diagonal_all(zl_):
-        return piece(W_ZF_ALL, wo_ref.at[c], wall.at[0, zl_, c], zf)
+    def w_diagonal_all(zl_, k):
+        both = pl.ds(k, 2)
+        return piece(W_ZF_ALL + k // 2 * (W_MESSAGES - 1 - W_ZF_ALL), wo_ref.at[c, both], wall.at[0, zl_, c, both], zf)
 
     def w_along(number, dy, z, k, device):
         return piece(number + 2 * (dy - 1) + z, held(dy, (zl + z) % 2, k), held(dy, (zl + z) % 2, k), device)
@@ -152,20 +159,23 @@
         w_spread(1, 0)
 
     def w_two():
+        for dy in (3, 1):
+            w_diagonal(dy, 1 - zl).wait_recv()
+            w_spread(dy, 1)
+        w_diagonal_all(zl, 0).start()
+
+    def w_three():
         w_forward(W_YP_FWD, 2, low, yp).wait_recv()
         w_forward(W_YM_FWD, 2, high, ym).wait_recv()
         w_diagonal(2, zl).start()
         w_spread(2, 0)
-        w_diagonal_all(zl).start()
-        for dy in (3, 1):
-            w_diagonal(dy, 1 - zl).wait_recv()
-            w_spread(dy, 1)
-
-    def w_three():
+        w_diagonal_all(zl, 2).start()
+
+    def w_four():
         w_diagonal(2, 1 - zl).wait_recv()
         w_spread(2, 1)
 
-    def w_four(z):
+    def w_five(z):
         for dy in (3, 1, 2):
             w_along(W_XP, dy, z, (x + 3) % 4, xp).wait_recv()
             w_sibling(3, dy, z, c).start()
@@ -213,59 +223,82 @@
         w_one()
         forward_up(0)
         forward_down(3)
+        message(Z_ABOVE, 3, above, zp).start()
         peer(0)
-        peer(3)
+        w_two()
+        arrive(Z_OWN, 3, across)
         forward_up(1)
         forward_down(2)
         peer(1)
         peer(2)
         arrive(YP_OWN, 2, below)
         arrive(YP_OWN, 3, below)
+        message(Z_BELOW, 3, below, zp).start()
 
     def third():
-        w_two()
         arrive(YM_OWN, 1, above)
         arrive(YM_OWN, 0, above)
+
+    def fourth():
+        w_three()
 
     def fifth():
         opposite(YP_FWD, 0)
         opposite(YM_FWD, 3)
         opposite(YP_FWD, 1)
         opposite(YM_FWD, 2)
-        w_three()
-
-    def sixth():
-        for k in range(CHUNKS):
-            arrive(YP_PEER, k, slot_of(3, 1))
-
-    def seventh():
-        for k in range(CHUNKS):
-            arrive(YM_PEER, k, slot_of(1, 1))
-
-    def eighth():
-        for k in range(CHUNKS):
-            arrive(Z_OPP, k, slot_of(2, 1))
-
-    order = (
-        (0, 0, None), (3, 0, second), (1, 0, third), (0, 1, None),
-        (2, 0, fifth), (3, 1, sixth), (1, 1, seventh), (2, 1, eighth),
-    )
+
+    last = ((3, YP_PEER), (1, YM_PEER), (2, Z_OPP))
+
+    def last_early():
+        w_four()
+        for dy, number in last:
+            arrive(number, 0, slot_of(dy, 1))
+            arrive(number, 3, slot_of(dy, 1))
+
+    def last_late():
+        for dy, number in last:
+            arrive(number, 1, slot_of(dy, 1))
+            arrive(number, 2, slot_of(dy, 1))
+
+    order = ((0, 0, None), (3, 0, second), (1, 0, third), (0, 1, fourth), (2, 0, fifth))
 
     def slice_rows(s):
         return pl.ds(pl.multiple_of(s * rows, rows), rows)
 
-    def halo(s, slot, number, device):
+    def halo(s, k, slot, number, device):
+        rows_ = slice_rows(s) if k is None else pl.ds(pl.multiple_of(s * rows + k * part, part), part)
+        sem = number + CHUNKS * s + (0 if k is None else k)
         return pltpu.make_async_remote_copy(
-            src_ref=kvbuf.at[slice_rows(s)], dst_ref=kv_out.at[slot, slice_rows(s)],
-            send_sem=halo_send.at[number + s], recv_sem=halo_recv.at[number + s],
-            device_id=device, device_id_type=MESH,
-        )
+            src_ref=kvbuf.at[rows_], dst_ref=kv_out.at[slot, rows_], send_sem=halo_send.at[sem],
+            recv_sem=halo_recv.at[sem], device_id=device, device_id_type=MESH,
+        )
+
+    def halos(s, k):
+        return halo(s, k, 2, CHUNKS * SLICES, xn), halo(s, k, 1, 0, sibling)
 
     def out_copies(s):
         return (
             pltpu.make_async_copy(qbuf.at[slice_rows(s)], q_out.at[slice_rows(s)], out_sem.at[s]),
             pltpu.make_async_copy(kvbuf.at[slice_rows(s)], kv_out.at[0, slice_rows(s)], out_sem.at[SLICES + s]),
         )
+
+    def slice_of(dy, dz, flip_):
+        return (y + dy) % 4 * 2 + (zl + dz + flip_) % 2
+
+    q_gain = qg_ref[...] * QSCALE
+
+    def put(mixed, spans):
+        for h in range(heads):
+            at = h * 3 * HD
+            query = head_norm(mixed[:, at : at + HD], q_gain)
+            key = head_norm(mixed[:, at + HD : at + 2 * HD], kg_ref[...])
+            value = mixed[:, at + 2 * HD : at + 3 * HD].astype(jnp.bfloat16)
+            for first, count, here in spans:
+                taken = slice(first, first + count)
+                qbuf[here, h * HD : (h + 1) * HD] = query[taken]
+                kvbuf[here, h * HD : (h + 1) * HD] = key[taken]
+                kvbuf[here, (heads + h) * HD : (heads + h + 1) * HD] = value[taken]
 
     def step(n, carry):
         dy, dz = jnp.int32(0), jnp.int32(0)
@@ -274,32 +307,43 @@
             dz = jnp.where(n == k, two, dz)
             if handler is not None:
                 pl.when(n == k)(handler)
-        slot = slot_of(dy, dz)
-        s = (y + dy) % 4 * 2 + (zl + dz + flip) % 2
-        here = slice_rows(s)
-
-        def head(h, carry):
-            mixed = jnp.dot(xbuf[slot], w[h], preferred_element_type=jnp.float32)
-            cols = pl.ds(pl.multiple_of(h * HD, HD), HD)
-            values = pl.ds(pl.multiple_of((heads + h) * HD, HD), HD)
-            qbuf[here, cols] = head_norm(mixed[:, :HD], qg_ref[...])
-            kvbuf[here, cols] = head_norm(mixed[:, HD : 2 * HD], kg_ref[...])
-            kvbuf[here, values] = mixed[:, 2 * HD :].astype(jnp.bfloat16)
-            return carry
-
-        lax.fori_loop(0, heads, head, 0)
-        halo(s, 2, SLICES, xn).start()
-        halo(s, 1, 0, sibling).start()
-        for copy in out_copies(s):
+        s = slice_of(dy, dz, flip)
+        put(jnp.dot(xbuf[slot_of(dy, dz)], w[...], preferred_element_type=jnp.float32), ((0, rows, slice_rows(s)),))
+        for copy in halos(s, None) + out_copies(s):
             copy.start()
         return carry
 
-    w_copy.wait()
-    lax.fori_loop(0, SLICES, step, 0)
-    w_diagonal_all(1 - zl).wait_recv()
+    for copy in w_copies:
+        copy.wait()
+    lax.fori_loop(0, len(order), step, 0)
+
+    def last_step(n, carry):
+        pl.when(n == 0)(last_early)
+        pl.when(n == 1)(last_late)
+        chunks = (n, 3 - n)
+        taken, spans = [], []
+        for dy, _ in last:
+            s = slice_of(dy, 1, flip)
+            for k in chunks:
+                spans.append((len(taken) * part, part, pl.ds(pl.multiple_of(s * rows + k * part, part), part)))
+                taken.append(xbuf[slot_of(dy, 1), pl.ds(pl.multiple_of(k * part, part), part), :])
+        put(jnp.dot(jnp.concatenate(taken, axis=0), w[...], preferred_element_type=jnp.float32), spans)
+        for dy, _ in last:
+            s = slice_of(dy, 1, flip)
+            for k in chunks:
+                for copy in halos(s, k):
+                    copy.start()
+        return carry
+
+    lax.fori_loop(0, 2, last_step, 0)
+    for dy, _ in last:
+        for copy in out_copies(slice_of(dy, 1, flip)):
+            copy.start()
+    w_diagonal_all(1 - zl, 0).wait_recv()
+    w_diagonal_all(1 - zl, 2).wait_recv()
     w_sibling_all(c).start()
-    w_four(0)
-    w_four(1)
+    w_five(0)
+    w_five(1)
 
     @pl.when(flip == 1)
     def _():
@@ -311,19 +355,27 @@
         for k in ks:
             message(number, k, pos, zp).wait_send()
 
-    def finish(s, carry):
-        for copy in out_copies(s):
+    for dy, dz in [one[:2] for one in order]:
+        for copy in out_copies(slice_of(dy, dz, flip)):
             copy.wait()
-        halo(s, 1, 0, sibling).wait()
-        halo(s, 2, SLICES, xn).wait()
-        return carry
-
-    lax.fori_loop(0, SLICES, finish, 0)
+        for copy in halos(slice_of(dy, dz, flip), None):
+            copy.wait_send()
+        for copy in halos(slice_of(dy, dz, 1 - flip), None):
+            copy.wait_recv()
+    for dy, _ in last:
+        for copy in out_copies(slice_of(dy, 1, flip)):
+            copy.wait()
+        for k in range(CHUNKS):
+            for copy in halos(slice_of(dy, 1, flip), k):
+                copy.wait_send()
+            for copy in halos(slice_of(dy, 1, 1 - flip), k):
+                copy.wait_recv()
     w_first(W_YP, 3, yp).wait_send()
     w_first(W_YM, 1, ym).wait_send()
     w_forward(W_YP_FWD, 2, low, yp).wait_send()
     w_forward(W_YM_FWD, 2, high, ym).wait_send()
-    w_diagonal_all(zl).wait_send()
+    w_diagonal_all(zl, 0).wait_send()
+    w_diagonal_all(zl, 2).wait_send()
     w_sibling_all(1 - c).wait()
     for dy in (1, 2, 3):
         w_diagonal(dy, zl).wait_send()
@@ -354,16 +406,16 @@
         scratch_shapes=[
             pltpu.VMEM((SLICES, rows, depth), jnp.bfloat16),
             pltpu.VMEM((rows, depth), jnp.bfloat16),
-            pltpu.VMEM(w.shape, jnp.bfloat16),
+            pltpu.VMEM((depth, 3 * width), jnp.bfloat16),
             pltpu.VMEM((SLICES * rows, width), jnp.bfloat16),
             pltpu.VMEM((SLICES * rows, 2 * width), jnp.bfloat16),
-            dma((MESSAGES,)), dma((MESSAGES,)), dma((2 * SLICES,)), dma((2 * SLICES,)), dma((2 * SLICES,)), dma(()),
+            dma((MESSAGES,)), dma((MESSAGES,)), dma((2 * CHUNKS * SLICES,)), dma((2 * CHUNKS * SLICES,)), dma((2 * SLICES,)), dma((heads,)),
             dma((W_MESSAGES,)), dma((W_MESSAGES,)),
         ],
         compiler_params=pltpu.CompilerParams(
             vmem_limit_bytes=VMEM_LIMIT, collective_id=0, has_side_effects=True
         ),
-    )(tokens, (1.0 + mod_scale)[None], shift[None], w, (q_gain * QSCALE)[None], k_gain[None], w_out)
+    )(tokens, mod_scale[None], shift[None], w, q_gain[None], k_gain[None], w_out)
 
 
 def attention_kernel(heads, pat_ref, cnt_ref, t_ref, q_ref, kv_ref, out_ref, kwin, vwin, vext, acc, todo, sem):
@@ -374,7 +426,9 @@
     for o in range(3):
         for part, into in ((0, kwin), (1, vwin)):
             copy = pltpu.make_async_copy(
-                kv_ref.at[slots[o], :, part * width : (part + 1) * width], into.at[o], sem.at[2 * o + part]
+                kv_ref.at[slots[o], :, :, part * width : (part + 1) * width],
+                into.at[o * GS : (o + 1) * GS],
+                sem.at[2 * o + part],
             )
             copy.start()
             copies.append(copy)
@@ -384,16 +438,19 @@
         for o in range(3):
             inside = (t + o - 1 >= 0) & (t + o - 1 < NT)
             for j in range(GS):
-                todo[i * 13 + 1 + count] = o * GS + j
-                live = inside & (pat_ref[(o * GS + i) * GS + j] > 0)
+                todo[i * 14 + 1 + count] = o * GS + j
+                live = inside & (pat_ref[o, i, j] > 0)
                 count = count + live.astype(jnp.int32)
-        todo[i * 13] = count
+        todo[i * 14 + 1 + count] = NONE
+        todo[i * 14] = (count + 1) // 2
         return carry
 
     lax.fori_loop(0, GS, list_tile, 0)
     for copy in copies:
         copy.wait()
 
+    kwin[NONE] = jnp.zeros_like(kwin[NONE])
+    vext[NONE] = jnp.zeros_like(vext[NONE])
     place = lax.broadcasted_iota(jnp.int32, (TILE, HD), 0)
     for o in range(3):
         valid = cnt_ref[jnp.clip(t + o - 1, 0, NT - 1)]
@@ -401,12 +458,11 @@
         ones = jnp.where(keep, 1.0, 0.0).astype(jnp.bfloat16)
 
         def fill(j, carry):
-            rows = pl.ds(pl.multiple_of(j * TILE, TILE), TILE)
             for h in range(heads):
-                vext[o, rows, 2 * h * HD : (2 * h + 1) * HD] = (
-                    vwin[o, rows, h * HD : (h + 1) * HD] * ones
+                vext[o * GS + j, :, 2 * h * HD : (2 * h + 1) * HD] = (
+                    vwin[o * GS + j, :, h * HD : (h + 1) * HD] * ones
                 )
-                vext[o, rows, (2 * h + 1) * HD : (2 * h + 2) * HD] = ones
+                vext[o * GS + j, :, (2 * h + 1) * HD : (2 * h + 2) * HD] = ones
             return carry
 
         lax.fori_loop(0, GS, fill, 0)
@@ -416,23 +472,24 @@
         acc[...] = jnp.zeros_like(acc)
 
         def pair(n, carry):
-            which = todo[i * 13 + 1 + n]
-            o = which // GS
-            keys = pl.ds(pl.multiple_of((which % GS) * TILE, TILE), TILE)
+            both = (todo[i * 14 + 1 + 2 * n], todo[i * 14 + 2 + 2 * n])
+            probs = []
             for h in range(heads):
+                cols = slice(h * HD, (h + 1) * HD)
                 score = lax.dot_general(
-                    q_ref[mine, h * HD : (h + 1) * HD],
-                    kwin[o, keys, h * HD : (h + 1) * HD],
+                    q_ref[mine, cols],
+                    jnp.concatenate([kwin[one, :, cols] for one in both], axis=0),
                     (((1,), (1,)), ((), ())),
                     preferred_element_type=jnp.float32,
                 )
-                prob = jnp.exp2(score).astype(jnp.bfloat16)
-                acc[h] += jnp.dot(
-                    prob, vext[o, keys, 2 * h * HD : (2 * h + 2) * HD], preferred_element_type=jnp.float32
-                )
+                probs.append(jnp.exp2(score).astype(jnp.bfloat16))
+            for h in range(heads):
+                cols = slice(2 * h * HD, (2 * h + 2) * HD)
+                values = jnp.concatenate([vext[one, :, cols] for one in both], axis=0)
+                acc[h] += jnp.dot(probs[h], values, preferred_element_type=jnp.float32)
             return carry
 
-        lax.fori_loop(0, todo[i * 13], pair, 0)
+        lax.fori_loop(0, todo[i * 14], pair, 0)
         for h in range(heads):
             out_ref[mine, h * HD : (h + 1) * HD] = (acc[h, :, :HD] / acc[h, :, HD:]).astype(jnp.bfloat16)
         return carry
@@ -453,22 +510,22 @@
         in_specs=[smem, smem, smem, vmem, hbm],
         out_specs=vmem,
         scratch_shapes=[
-            pltpu.VMEM((3, rows, width), jnp.bfloat16),
-            pltpu.VMEM((3, rows, width), jnp.bfloat16),
-            pltpu.VMEM((3, rows, 2 * width), jnp.bfloat16),
+            pltpu.VMEM((NONE + 1, TILE, width), jnp.bfloat16),
+            pltpu.VMEM((NONE, TILE, width), jnp.bfloat16),
+            pltpu.VMEM((NONE + 1, TILE, 2 * width), jnp.bfloat16),
             pltpu.VMEM((heads, TILE, 2 * HD), jnp.float32),
-            pltpu.SMEM((GS * 13 + 4,), jnp.int32),
+            pltpu.SMEM((GS * 14,), jnp.int32),
             pltpu.SemaphoreType.DMA((6,)),
         ],
         compiler_params=pltpu.CompilerParams(vmem_limit_bytes=VMEM_LIMIT),
-    )(pattern.reshape(-1), counts, t.reshape(1), q, kv)
-
-
-def finish_kernel(attn, tok_ref, gate_ref, wo_ref, wall, out_ref, rows_in, wv, acc, a_send, a_recv, x_send, x_recv, s_send, s_recv, w_sem, own_sem):
+    )(pattern, counts, t.reshape(1), q, kv.reshape(3, GS, TILE, 2 * width))
+
+
+def finish_kernel(attn, wo_ref, wall, out_ref, rows_in, wv, a_send, a_recv, x_send, x_recv, s_send, s_recv, w_sem, own_sem):
     x, zh, y, zl, c = place()
     nx = lax.axis_size("frame") // 2
-    rows = tok_ref.shape[0]
-    depth = tok_ref.shape[1]
+    rows, depth = out_ref.shape
+    width = attn.shape[1]
     pos = y * 2 + zl
     straight = zh == c
     sibling = {"rep": 1 - c}
@@ -506,15 +563,19 @@
             load(dy, (x + which) % 4).start()
     pl.semaphore_wait(barrier, jnp.where(straight, SLICES + 2, SLICES + 3))
 
+    def landing(source):
+        cols = pl.ds(pl.multiple_of(source % 2 * width, width), width)
+        return rows_in.at[source // 2, :, cols]
+
     def hand_out(s, source):
         return pltpu.make_async_remote_copy(
-            src_ref=attn.at[pl.ds(pl.multiple_of(s * rows, rows), rows)], dst_ref=rows_in.at[source],
+            src_ref=attn.at[pl.ds(pl.multiple_of(s * rows, rows), rows)], dst_ref=landing(source),
             send_sem=a_send.at[s], recv_sem=a_recv.at[source], device_id=owner(s), device_id_type=MESH,
         )
 
     def keep():
         return pltpu.make_async_copy(
-            attn.at[pl.ds(pl.multiple_of(pos * rows, rows), rows)], rows_in.at[pos], own_sem
+            attn.at[pl.ds(pl.multiple_of(pos * rows, rows), rows)], landing(pos), own_sem
         )
 
     def scatter(n, carry):
@@ -549,10 +610,9 @@
         far(0, dy, 0, (x + 3) % 4, xp).start()
         far(4, dy, 1, (x + 1) % 4, xm).start()
 
-    acc[...] = tok_ref[...].astype(jnp.float32)
     cols = min(512, depth)
 
-    def add(dy, z):
+    def arrived(dy, z):
         source = (y + dy) % 4 * 2 + (zl + z) % 2
         kept = jnp.logical_and(straight, source == pos)
 
@@ -564,17 +624,21 @@
         def _():
             hand_out(0, source).wait_recv()
 
+    def add(dy, first):
+        arrived(dy, 0)
+        arrived(dy, 1)
+
         def column(n, carry):
             here = pl.ds(pl.multiple_of(n * cols, cols), cols)
-            weight = wv[dy, (zl + z) % 2, :, :, :, here].reshape(rows_in.shape[2], cols)
-            acc[:, here] += gate_ref[:, here] * jnp.dot(rows_in[source], weight, preferred_element_type=jnp.float32)
+            weight = wv[dy, :, :, :, :, here].reshape(2 * width, cols)
+            term = jnp.dot(rows_in[(y + dy) % 4], weight, preferred_element_type=jnp.float32)
+            out_ref[:, here] = term if first else out_ref[:, here] + term
             return carry
 
         lax.fori_loop(0, depth // cols, column, 0)
 
     loads(lambda copy: copy.wait())
-    add(0, 0)
-    add(0, 1)
+    add(0, True)
     for dy in (1, 3, 2):
         far(0, dy, 0, (x + 2) % 4, xp).wait_recv()
         share(0, dy, 0, c).start()
@@ -584,9 +648,7 @@
             load(dy, (x + which) % 4).wait()
         share(0, dy, 0, 1 - c).wait_recv()
         share(4, dy, 1, 1 - c).wait_recv()
-        add(dy, 0)
-        add(dy, 1)
-    out_ref[...] = acc[...].astype(jnp.bfloat16)
+        add(dy, False)
 
     def sent(s, carry):
         @pl.when(others(s))
@@ -603,27 +665,27 @@
         share(4, dy, 1, c).wait_send()
 
 
-def finish(attn, tokens, gate, w_out, wall):
-    rows, depth = tokens.shape
+def finish(attn, rows, w_out, wall):
+    width = attn.shape[1]
+    depth = wall.shape[-1]
     vmem = pl.BlockSpec(memory_space=pltpu.VMEM)
     hbm = pl.BlockSpec(memory_space=pl.ANY)
     dma = pltpu.SemaphoreType.DMA
     return pl.pallas_call(
         finish_kernel,
         name="finish",
-        out_shape=jax.ShapeDtypeStruct((rows, depth), jnp.bfloat16),
-        in_specs=[hbm, vmem, vmem, hbm, hbm],
+        out_shape=jax.ShapeDtypeStruct((rows, depth), jnp.float32),
+        in_specs=[hbm, hbm, hbm],
         out_specs=vmem,
         scratch_shapes=[
-            pltpu.VMEM((SLICES, rows, attn.shape[1]), jnp.bfloat16),
+            pltpu.VMEM((SLICES // 2, rows, 2 * width), jnp.bfloat16),
             pltpu.VMEM(wall.shape, jnp.bfloat16),
-            pltpu.VMEM((rows, depth), jnp.float32),
             dma((SLICES,)), dma((SLICES,)), dma((8,)), dma((8,)), dma((8,)), dma((8,)), dma((16,)), dma(()),
         ],
         compiler_params=pltpu.CompilerParams(
             vmem_limit_bytes=VMEM_LIMIT, collective_id=1, has_side_effects=True
         ),
-    )(attn, tokens, gate[None], w_out, wall)
+    )(attn, w_out, wall)
 
 
 def per_device(tokens, shift, mod_scale, gate, w_qkv, q_gain, k_gain, w_out, pattern, counts):
@@ -631,7 +693,8 @@
     q, kv, wall = gather_project(tokens, shift, mod_scale, jnp.transpose(w_qkv, (1, 0, 2)), q_gain, k_gain, w_parts)
     block = lax.axis_index("frame") // 2 * 2 + lax.axis_index("rep")
     attn = attention(q, kv, pattern, counts, block)
-    return finish(attn, tokens, gate, w_parts, wall)
+    result = finish(attn, tokens.shape[0], w_parts, wall)
+    return (tokens.astype(jnp.float32) + gate * result).astype(jnp.bfloat16)
 
 
 def solution(mesh):

time: 179 us -> 153 us (0.85)
  the two profiles are of different devices: /device:TPU:24 before, /device:TPU:43 now
where the time goes in v4:
time: 153 us
  Pallas kernels  150 us (98%)
  other arithmetic  3 us (2%)
    pallas_call x1, Pallas kernels, gather_project(): pl.pallas_call(functools.partial(gather_kernel, heads), name='gather_proj...  88.1 us
    pallas_call x1, Pallas kernels, finish(): pl.pallas_call(finish_kernel, name='finish', out_shape=jax.ShapeDtypeStru...  38.4 us
    pallas_call x1, Pallas kernels, attention(): pl.pallas_call(functools.partial(attention_kernel, heads), name='attentio...  23.6 us

profile of v4, /device:TPU:43, one launch (start us, length us, event | category | flops | bytes accessed | tf_op | source)
XLA Modules:
  0.0 153.1 jit_solution(3174368214824990684)
XLA Ops:
  0.0 88.1 %gather_project.1 = (bf16[1536,384]{1,0:T(8,128)(2,1)}, bf16[3,1536,768]{2,1,0:T(8,128)(2,1)}, bf16[4,2,2,4,48,3072]{5,4,3,2,1,0:T(8,128)(2,1)}) custom-call(bf16[192,3072]{1,0:T(8,128)(2,1)} %tok_ref.1, f32[1,3072]{1,0:T(1,128)} %bitcast.12, f32[1,3072]{1,0:T(1,128)} %bitcast.13, bf16[3,3072,384]{2,1,0:T(8,128)(2,1)} %bitcast.10, f32[1,128]{1,0:T(1,128)} %bitcast.14, ...), custom_call_target="tpu_custom_call" | custom-call | tf_op jit(solution)/shard_map/gather_project/pallas_call | solution.py:396
  88.1 23.6 %attention.1.attn = bf16[1536,384]{1,0:T(8,128)(2,1)} custom-call(s32[3,4,4]{2,1,0:T(4,128)} %pat_ref.1, s32[8]{0:T(128)} %cnt_ref.1, s32[1]{0:T(128)} %bitcast.t_ref, bf16[1536,384]{1,0:T(8,128)(2,1)} %get-tuple-element.8.q_ref, bf16[3,4,384,768]{3,2,1,0:T(8,128)(2,1)} %bitcast.11), custom_call_target="tpu_custom_call" | custom-call | tf_op jit(solution)/shard_map/attention/pallas_call | solution.py:506
  111.7 0.0 copy-start
  111.7 0.0 copy-start.1
  111.7 38.4 %finish.1 = f32[192,3072]{1,0:T(8,128)} custom-call(bf16[1536,384]{1,0:T(8,128)(2,1)} %attention.1.attn, bf16[2,4,48,3072]{3,2,1,0:T(8,128)(2,1)} %bitcast.9, bf16[4,2,2,4,48,3072]{5,4,3,2,1,0:T(8,128)(2,1)} %get-tuple-element.10.wall), custom_call_target="tpu_custom_call" | custom-call | tf_op jit(solution)/shard_map/finish/pallas_call | solution.py:674
  150.1 0.0 copy-done
  150.1 0.0 copy-done.1
  150.1 3.0 %add_convert_fusion = bf16[192,3072]{1,0:T(8,128)(2,1)} fusion(f32[192,3072]{1,0:T(8,128)} %finish.1, bf16[192,3072]{1,0:T(8,128)(2,1)S(1)} %copy-done, f32[3072]{0:T(1024)S(1)} %copy-done.1), kind=kLoop, calls=%fused_computation | loop fusion | flops 2359296 | bytes 4730880 | tf_op jit(solution)/shard_map/convert_element_type | solution.py:697
Async XLA Ops:
  111.7 38.4 %copy-start = (bf16[192,3072]{1,0:T(8,128)(2,1)S(1)}, bf16[192,3072]{1,0:T(8,128)(2,1)}, u32[]{:S(2)}) copy-start(bf16[192,3072]{1,0:T(8,128)(2,1)} %tok_ref.1) | copy-start | bytes 3538948
  111.7 38.4 %copy-start.1 = (f32[3072]{0:T(1024)S(1)}, f32[3072]{0:T(1024)}, u32[]{:S(2)}) copy-start(f32[3072]{0:T(1024)} %param.13) | copy-start | bytes 36868

commit v5 on v4

--- a/solution.py
+++ b/solution.py
@@ -28,7 +28,7 @@
 Z_BELOW, Z_ABOVE = YP_PEER, YM_PEER
 MESSAGES = 36
 W_YP, W_YM, W_YP_FWD, W_YM_FWD, W_ZF, W_ZF_ALL, W_XP, W_XM, W_SIB, W_SIB_ALL = 0, 1, 2, 3, 4, 7, 8, 14, 20, 38
-W_MESSAGES = 40
+W_MESSAGES = 42
 SLICES = 8
 
 
@@ -69,7 +69,8 @@
         return pl.ds(k * part, part)
 
     scale = 1.0 + scale_ref[...]
-    for k in range(CHUNKS):
+
+    def normalise(k):
         values = tok_ref[chunk(k), :].astype(jnp.float32)
         center = jnp.mean(values, axis=-1, keepdims=True)
         centred = values - center
@@ -81,8 +82,6 @@
         def _():
             xbuf[pos, chunk(k), :] = normed
 
-    pl.semaphore_wait(barrier, len(neighbours))
-
     def slot_of(dy, dz):
         return (y + dy) % 4 * 2 + (zl + dz) % 2
 
@@ -99,11 +98,6 @@
             recv_sem=recv.at[SWAP + k], device_id=partner, device_id_type=MESH,
         )
 
-    @pl.when(flip == 1)
-    def _():
-        for k in (0, 3, 1, 2):
-            swap(k, y * 2 + 1 - zl).start()
-
     half = wo_ref.shape[-1] // 2
 
     def piece(number, src, dst, device):
@@ -135,9 +129,13 @@
         there = wall.at[dy, (zl + z) % 2, core, (x + which) % 4]
         return piece(W_SIB + 6 * {0: 0, 1: 1, 3: 2}[which] + 2 * (dy - 1) + z, there, there, sibling)
 
-    def w_sibling_all(core):
-        there = wall.at[0, 1 - zl, core]
-        return piece(W_SIB_ALL, there, there, sibling)
+    def w_sibling_all(core, k):
+        there = wall.at[0, 1 - zl, core, pl.ds(k, 2)]
+        return piece(W_SIB_ALL + k, there, there, sibling)
+
+    def w_half(k):
+        w_diagonal_all(1 - zl, k).wait_recv()
+        w_sibling_all(c, k).start()
 
     def w_spread(dy, z):
         w_along(W_XP, dy, z, x, xp).start()
@@ -145,8 +143,6 @@
         w_sibling(0, dy, z, c).start()
 
     low, high = pl.ds(0, half), pl.ds(half, half)
-    w_first(W_YP, 3, yp).start()
-    w_first(W_YM, 1, ym).start()
 
     def w_one():
         w_first(W_YP, 3, yp).wait_recv()
@@ -189,23 +185,41 @@
         for k in ks:
             message(number, k, pos, device).start()
 
-    for k, to_yp, to_ym in ((0, (0,), ()), (3, (), (3,)), (1, (1,), ()), (2, (), (2,))):
-        @pl.when(flip == 1)
-        def _():
-            swap(k, pos).wait_recv()
-
+    def own_out(k, to_yp, to_ym):
         own(Z_OWN, (k,), zp)
         own(YP_OWN, to_yp, yp)
         own(YM_OWN, to_ym, ym)
-    own(YP_OWN, (2, 3), yp)
-    own(YM_OWN, (1, 0), ym)
+
+    first_out = ((0, (0,), ()), (3, (), (3,)), (1, (1,), ()), (2, (), (2,)))
+    for k, to_yp, to_ym in first_out:
+        normalise(k)
+        if k == 0:
+            pl.semaphore_wait(barrier, len(neighbours))
+            w_first(W_YP, 3, yp).start()
+            w_first(W_YM, 1, ym).start()
+
+        @pl.when(flip == 1)
+        def _():
+            swap(k, y * 2 + 1 - zl).start()
+
+        @pl.when(flip == 0)
+        def _():
+            own_out(k, to_yp, to_ym)
+
+    @pl.when(flip == 1)
+    def _():
+        for k, to_yp, to_ym in first_out:
+            swap(k, pos).wait_recv()
+            own_out(k, to_yp, to_ym)
 
     below, above, across, facing = slot_of(3, 0), slot_of(1, 0), slot_of(0, 1), slot_of(2, 0)
 
     def peer(k):
         arrive(Z_OWN, k, across)
-        message(YP_PEER, k, across, yp).start()
-        message(YM_PEER, k, across, ym).start()
+        if k != 0:
+            message(YP_PEER, k, across, yp).start()
+        if k != 3:
+            message(YM_PEER, k, across, ym).start()
 
     def forward_up(k):
         arrive(YP_OWN, k, below)
@@ -222,46 +236,45 @@
     def second():
         w_one()
         forward_up(0)
+        message(Z_BELOW, 0, below, zp).start()
         forward_down(3)
         message(Z_ABOVE, 3, above, zp).start()
-        peer(0)
-        w_two()
-        arrive(Z_OWN, 3, across)
         forward_up(1)
         forward_down(2)
+        own(YP_OWN, (2, 3), yp)
+        own(YM_OWN, (1, 0), ym)
+        peer(0)
+        peer(3)
+        w_two()
         peer(1)
+        opposite(YP_FWD, 0)
+        opposite(YM_FWD, 3)
         peer(2)
+        w_three()
+        opposite(YP_FWD, 1)
+        opposite(YM_FWD, 2)
+        w_four()
+
+    def fourth():
         arrive(YP_OWN, 2, below)
         arrive(YP_OWN, 3, below)
-        message(Z_BELOW, 3, below, zp).start()
-
-    def third():
+
+    def fifth():
         arrive(YM_OWN, 1, above)
         arrive(YM_OWN, 0, above)
 
-    def fourth():
-        w_three()
-
-    def fifth():
-        opposite(YP_FWD, 0)
-        opposite(YM_FWD, 3)
-        opposite(YP_FWD, 1)
-        opposite(YM_FWD, 2)
-
     last = ((3, YP_PEER), (1, YM_PEER), (2, Z_OPP))
 
-    def last_early():
-        w_four()
-        for dy, number in last:
-            arrive(number, 0, slot_of(dy, 1))
-            arrive(number, 3, slot_of(dy, 1))
-
-    def last_late():
-        for dy, number in last:
-            arrive(number, 1, slot_of(dy, 1))
-            arrive(number, 2, slot_of(dy, 1))
-
-    order = ((0, 0, None), (3, 0, second), (1, 0, third), (0, 1, fourth), (2, 0, fifth))
+    def last_chunk(k):
+        def handler():
+            if k == 0:
+                w_half(0)
+            for dy, number in last:
+                arrive(number, k, slot_of(dy, 1))
+
+        return handler
+
+    order = ((0, 0, None), (0, 1, second), (2, 0, None), (3, 0, fourth), (1, 0, fifth))
 
     def slice_rows(s):
         return pl.ds(pl.multiple_of(s * rows, rows), rows)
@@ -318,30 +331,27 @@
     lax.fori_loop(0, len(order), step, 0)
 
     def last_step(n, carry):
-        pl.when(n == 0)(last_early)
-        pl.when(n == 1)(last_late)
-        chunks = (n, 3 - n)
+        k = jnp.int32(0)
+        for at, one in enumerate((0, 3, 1, 2)):
+            k = jnp.where(n == at, one, k)
+            pl.when(n == at)(last_chunk(one))
         taken, spans = [], []
         for dy, _ in last:
             s = slice_of(dy, 1, flip)
-            for k in chunks:
-                spans.append((len(taken) * part, part, pl.ds(pl.multiple_of(s * rows + k * part, part), part)))
-                taken.append(xbuf[slot_of(dy, 1), pl.ds(pl.multiple_of(k * part, part), part), :])
+            spans.append((len(taken) * part, part, pl.ds(pl.multiple_of(s * rows + k * part, part), part)))
+            taken.append(xbuf[slot_of(dy, 1), pl.ds(pl.multiple_of(k * part, part), part), :])
         put(jnp.dot(jnp.concatenate(taken, axis=0), w[...], preferred_element_type=jnp.float32), spans)
         for dy, _ in last:
             s = slice_of(dy, 1, flip)
-            for k in chunks:
-                for copy in halos(s, k):
-                    copy.start()
+            for copy in halos(s, k):
+                copy.start()
         return carry
 
-    lax.fori_loop(0, 2, last_step, 0)
+    lax.fori_loop(0, CHUNKS, last_step, 0)
     for dy, _ in last:
         for copy in out_copies(slice_of(dy, 1, flip)):
             copy.start()
-    w_diagonal_all(1 - zl, 0).wait_recv()
-    w_diagonal_all(1 - zl, 2).wait_recv()
-    w_sibling_all(c).start()
+    w_half(2)
     w_five(0)
     w_five(1)
 
@@ -376,7 +386,8 @@
     w_forward(W_YM_FWD, 2, high, ym).wait_send()
     w_diagonal_all(zl, 0).wait_send()
     w_diagonal_all(zl, 2).wait_send()
-    w_sibling_all(1 - c).wait()
+    w_sibling_all(1 - c, 0).wait()
+    w_sibling_all(1 - c, 2).wait()
     for dy in (1, 2, 3):
         w_diagonal(dy, zl).wait_send()
         for z in (0, 1):
@@ -418,7 +429,7 @@
     )(tokens, mod_scale[None], shift[None], w, q_gain[None], k_gain[None], w_out)
 
 
-def attention_kernel(heads, pat_ref, cnt_ref, t_ref, q_ref, kv_ref, out_ref, kwin, vwin, vext, acc, todo, sem):
+def attention_kernel(heads, pat_ref, cnt_ref, t_ref, q_ref, kv_ref, out_ref, kwin, vwin, ones, acc, todo, sem):
     t = t_ref[0]
     width = heads * HD
     slots = (2 - t % 2, 0, 1 + t % 2)
@@ -446,50 +457,62 @@
         return carry
 
     lax.fori_loop(0, GS, list_tile, 0)
+    kwin[NONE] = jnp.zeros_like(kwin[NONE])
+    vwin[NONE] = jnp.zeros_like(vwin[NONE])
+    ones[3] = jnp.zeros_like(ones[3])
+    place = lax.broadcasted_iota(jnp.int32, (TILE, HD), 0)
+    for o in range(3):
+        ones[o] = jnp.where(place < cnt_ref[jnp.clip(t + o - 1, 0, NT - 1)], 1.0, 0.0).astype(jnp.bfloat16)
     for copy in copies:
         copy.wait()
 
-    kwin[NONE] = jnp.zeros_like(kwin[NONE])
-    vext[NONE] = jnp.zeros_like(vext[NONE])
-    place = lax.broadcasted_iota(jnp.int32, (TILE, HD), 0)
     for o in range(3):
-        valid = cnt_ref[jnp.clip(t + o - 1, 0, NT - 1)]
-        keep = place < valid
-        ones = jnp.where(keep, 1.0, 0.0).astype(jnp.bfloat16)
-
-        def fill(j, carry):
-            for h in range(heads):
-                vext[o * GS + j, :, 2 * h * HD : (2 * h + 1) * HD] = (
-                    vwin[o * GS + j, :, h * HD : (h + 1) * HD] * ones
-                )
-                vext[o * GS + j, :, (2 * h + 1) * HD : (2 * h + 2) * HD] = ones
-            return carry
-
-        lax.fori_loop(0, GS, fill, 0)
+        @pl.when(cnt_ref[jnp.clip(t + o - 1, 0, NT - 1)] < TILE)
+        def _():
+            def clear(j, carry):
+                for h in range(heads):
+                    cols = slice(h * HD, (h + 1) * HD)
+                    vwin[o * GS + j, :, cols] = vwin[o * GS + j, :, cols] * ones[o]
+                return carry
+
+            lax.fori_loop(0, GS, clear, 0)
 
     def tile(i, carry):
         mine = pl.ds(pl.multiple_of(i * TILE, TILE), TILE)
         acc[...] = jnp.zeros_like(acc)
 
-        def pair(n, carry):
-            both = (todo[i * 14 + 1 + 2 * n], todo[i * 14 + 2 + 2 * n])
+        def attend(which):
             probs = []
             for h in range(heads):
                 cols = slice(h * HD, (h + 1) * HD)
                 score = lax.dot_general(
                     q_ref[mine, cols],
-                    jnp.concatenate([kwin[one, :, cols] for one in both], axis=0),
+                    jnp.concatenate([kwin[one, :, cols] for one in which], axis=0),
                     (((1,), (1,)), ((), ())),
                     preferred_element_type=jnp.float32,
                 )
                 probs.append(jnp.exp2(score).astype(jnp.bfloat16))
+            valid = jnp.concatenate([ones[one // GS] for one in which], axis=0)
             for h in range(heads):
-                cols = slice(2 * h * HD, (2 * h + 2) * HD)
-                values = jnp.concatenate([vext[one, :, cols] for one in both], axis=0)
-                acc[h] += jnp.dot(probs[h], values, preferred_element_type=jnp.float32)
+                cols = slice(h * HD, (h + 1) * HD)
+                values = jnp.concatenate([vwin[one, :, cols] for one in which], axis=0)
+                acc[h] += jnp.dot(
+                    probs[h], jnp.concatenate([values, valid], axis=1), preferred_element_type=jnp.float32
+                )
+
+        pairs = todo[i * 14]
+        first = i * 14 + 1
+
+        def four(n, carry):
+            attend([todo[first + 4 * n + m] for m in range(4)])
             return carry
 
-        lax.fori_loop(0, todo[i * 14], pair, 0)
+        lax.fori_loop(0, pairs // 2, four, 0)
+
+        @pl.when(pairs % 2 == 1)
+        def _():
+            attend([todo[first + 2 * (pairs - 1) + m] for m in range(2)])
+
         for h in range(heads):
             out_ref[mine, h * HD : (h + 1) * HD] = (acc[h, :, :HD] / acc[h, :, HD:]).astype(jnp.bfloat16)
         return carry
@@ -511,8 +534,8 @@
         out_specs=vmem,
         scratch_shapes=[
             pltpu.VMEM((NONE + 1, TILE, width), jnp.bfloat16),
-            pltpu.VMEM((NONE, TILE, width), jnp.bfloat16),
-            pltpu.VMEM((NONE + 1, TILE, 2 * width), jnp.bfloat16),
+            pltpu.VMEM((NONE + 1, TILE, width), jnp.bfloat16),
+            pltpu.VMEM((GS, TILE, HD), jnp.bfloat16),
             pltpu.VMEM((heads, TILE, 2 * HD), jnp.float32),
             pltpu.SMEM((GS * 14,), jnp.int32),
             pltpu.SemaphoreType.DMA((6,)),
@@ -578,26 +601,30 @@
             attn.at[pl.ds(pl.multiple_of(pos * rows, rows), rows)], landing(pos), own_sem
         )
 
-    def scatter(n, carry):
-        s = (pos + n) % SLICES
-
-        @pl.when(others(s))
-        def _():
-            hand_out(s, pos).start()
-
-        return carry
-
-    lax.fori_loop(0, SLICES, scatter, 0)
-
-    @pl.when(straight)
-    def _():
-        keep().start()
-
     def far(number, dy, z, k, device):
         return pltpu.make_async_remote_copy(
             src_ref=wall.at[dy, z, c, k], dst_ref=wv.at[dy, z, c, k], send_sem=x_send.at[number + dy],
             recv_sem=x_recv.at[number + dy], device_id=device, device_id_type=MESH,
         )
+
+    def scatter(n, carry):
+        ahead = jnp.where(n < 4, n // 2, 5 - n // 2)
+        s = (y + ahead) % 4 * 2 + (zl + n) % 2
+
+        @pl.when(others(s))
+        def _():
+            hand_out(s, pos).start()
+
+        return carry
+
+    for dy in (1, 3, 2):
+        far(0, dy, 0, (x + 3) % 4, xp).start()
+        far(4, dy, 1, (x + 1) % 4, xm).start()
+    lax.fori_loop(0, SLICES, scatter, 0)
+
+    @pl.when(straight)
+    def _():
+        keep().start()
 
     def share(number, dy, z, core):
         there = wv.at[dy, z, core, (x + 2) % 4]
@@ -606,11 +633,7 @@
             device_id=sibling, device_id_type=MESH,
         )
 
-    for dy in (1, 3, 2):
-        far(0, dy, 0, (x + 3) % 4, xp).start()
-        far(4, dy, 1, (x + 1) % 4, xm).start()
-
-    cols = min(512, depth)
+    cols = depth
 
     def arrived(dy, z):
         source = (y + dy) % 4 * 2 + (zl + z) % 2

time: 153 us -> 148 us (0.967)
  the two profiles are of different devices: /device:TPU:43 before, /device:TPU:1 now
where the time goes in v5:
time: 148 us
  Pallas kernels  145 us (98%)
  other arithmetic  3 us (2%)
    pallas_call x1, Pallas kernels, gather_project(): pl.pallas_call(functools.partial(gather_kernel, heads), name='gather_proj...  89.8 us
    pallas_call x1, Pallas kernels, finish(): pl.pallas_call(finish_kernel, name='finish', out_shape=jax.ShapeDtypeStru...  33.7 us
    pallas_call x1, Pallas kernels, attention(): pl.pallas_call(functools.partial(attention_kernel, heads), name='attentio...  21.1 us
    convert_element_type x1, other arithmetic, per_device(): return (tokens.astype(jnp.float32) + gate * result).astype(jnp.bfloat16)  3 us

profile of v5, /device:TPU:1, one launch (start us, length us, event | category | flops | bytes accessed | tf_op | source)
XLA Modules:
  0.0 147.7 jit_solution(17644730143215091266)
XLA Ops:
  0.0 89.8 %gather_project.1 = (bf16[1536,384]{1,0:T(8,128)(2,1)}, bf16[3,1536,768]{2,1,0:T(8,128)(2,1)}, bf16[4,2,2,4,48,3072]{5,4,3,2,1,0:T(8,128)(2,1)}) custom-call(bf16[192,3072]{1,0:T(8,128)(2,1)} %tok_ref.1, f32[1,3072]{1,0:T(1,128)} %bitcast.12, f32[1,3072]{1,0:T(1,128)} %bitcast.13, bf16[3,3072,384]{2,1,0:T(8,128)(2,1)} %bitcast.10, f32[1,128]{1,0:T(1,128)} %bitcast.14, ...), custom_call_target="tpu_custom_call" | custom-call | tf_op jit(solution)/shard_map/gather_project/pallas_call | solution.py:407
  89.9 21.1 %attention.1.attn = bf16[1536,384]{1,0:T(8,128)(2,1)} custom-call(s32[3,4,4]{2,1,0:T(4,128)} %pat_ref.1, s32[8]{0:T(128)} %cnt_ref.1, s32[1]{0:T(128)} %bitcast.t_ref, bf16[1536,384]{1,0:T(8,128)(2,1)} %get-tuple-element.8.q_ref, bf16[3,4,384,768]{3,2,1,0:T(8,128)(2,1)} %bitcast.11), custom_call_target="tpu_custom_call" | custom-call | tf_op jit(solution)/shard_map/attention/pallas_call | solution.py:529
  111.0 0.0 copy-start
  111.0 0.0 copy-start.1
  111.0 33.7 %finish.1 = f32[192,3072]{1,0:T(8,128)} custom-call(bf16[1536,384]{1,0:T(8,128)(2,1)} %attention.1.attn, bf16[2,4,48,3072]{3,2,1,0:T(8,128)(2,1)} %bitcast.9, bf16[4,2,2,4,48,3072]{5,4,3,2,1,0:T(8,128)(2,1)} %get-tuple-element.10.wall), custom_call_target="tpu_custom_call" | custom-call | tf_op jit(solution)/shard_map/finish/pallas_call | solution.py:697
  144.7 0.0 copy-done
  144.7 0.0 copy-done.1
  144.7 3.0 %add_convert_fusion = bf16[192,3072]{1,0:T(8,128)(2,1)} fusion(f32[192,3072]{1,0:T(8,128)} %finish.1, bf16[192,3072]{1,0:T(8,128)(2,1)S(1)} %copy-done, f32[3072]{0:T(1024)S(1)} %copy-done.1), kind=kLoop, calls=%fused_computation | loop fusion | flops 2359296 | bytes 4730880 | tf_op jit(solution)/shard_map/convert_element_type | solution.py:720
Async XLA Ops:
  111.0 33.7 %copy-start = (bf16[192,3072]{1,0:T(8,128)(2,1)S(1)}, bf16[192,3072]{1,0:T(8,128)(2,1)}, u32[]{:S(2)}) copy-start(bf16[192,3072]{1,0:T(8,128)(2,1)} %tok_ref.1) | copy-start | bytes 3538948
  111.0 33.7 %copy-start.1 = (f32[3072]{0:T(1024)S(1)}, f32[3072]{0:T(1024)}, u32[]{:S(2)}) copy-start(f32[3072]{0:T(1024)} %param.13) | copy-start | bytes 36868

commit v6 on v5

--- a/solution.py
+++ b/solution.py
@@ -13,7 +13,7 @@
 NT = 8
 ROWS = GS * TILE
 NONE = 3 * GS
-VMEM_LIMIT = 56 * 1024 * 1024
+MIB = 1024 * 1024
 QSCALE = HD**-0.5 * 1.4426950408889634
 
 
@@ -37,8 +37,8 @@
     return f // 2, f % 2, h // 2, h % 2, c
 
 
-def gather_kernel(heads, tok_ref, scale_ref, shift_ref, w_hbm, qg_ref, kg_ref, wo_ref, q_out, kv_out, wall,
-                  xbuf, mine, w, qbuf, kvbuf, send, recv, halo_send, halo_recv, out_sem, w_sem, wo_send, wo_recv):
+def gather_kernel(heads, tok_hbm, scale_hbm, shift_hbm, w_hbm, qg_hbm, kg_hbm, wo_ref, q_out, kv_out, wall,
+                  tok_ref, scale_ref, shift_ref, qg_ref, kg_ref, in_sem, xbuf, mine, w, qbuf, kvbuf, send, recv, halo_send, halo_recv, out_sem, w_sem, wo_send, wo_recv):
     x, zh, y, zl, c = place()
     nx = lax.axis_size("frame") // 2
     rows = mine.shape[0]
@@ -59,6 +59,14 @@
     for device in neighbours:
         pl.semaphore_signal(barrier, inc=1, device_id=device, device_id_type=MESH)
 
+    in_copies = [
+        pltpu.make_async_copy(source, into, in_sem.at[n])
+        for n, (source, into) in enumerate((
+            (tok_hbm, tok_ref), (scale_hbm, scale_ref), (shift_hbm, shift_ref), (qg_hbm, qg_ref), (kg_hbm, kg_ref),
+        ))
+    ]
+    for copy in in_copies:
+        copy.start()
     w_copies = [
         pltpu.make_async_copy(w_hbm.at[h], w.at[:, h * 3 * HD : (h + 1) * 3 * HD], w_sem.at[h]) for h in range(heads)
     ]
@@ -68,6 +76,8 @@
     def chunk(k):
         return pl.ds(k * part, part)
 
+    for copy in in_copies:
+        copy.wait()
     scale = 1.0 + scale_ref[...]
 
     def normalise(k):
@@ -401,7 +411,6 @@
     rows, depth = tokens.shape
     heads = w.shape[0]
     width = heads * HD
-    vmem = pl.BlockSpec(memory_space=pltpu.VMEM)
     hbm = pl.BlockSpec(memory_space=pl.ANY)
     dma = pltpu.SemaphoreType.DMA
     return pl.pallas_call(
@@ -412,9 +421,15 @@
             jax.ShapeDtypeStruct((3, SLICES * rows, 2 * width), jnp.bfloat16),
             jax.ShapeDtypeStruct((4, 2) + w_out.shape, jnp.bfloat16),
         ),
-        in_specs=[vmem, vmem, vmem, hbm, vmem, vmem, hbm],
+        in_specs=[pl.BlockSpec(memory_space=pltpu.HBM)] * 7,
         out_specs=(hbm, hbm, hbm),
         scratch_shapes=[
+            pltpu.VMEM((rows, depth), jnp.bfloat16),
+            pltpu.VMEM((1, depth), jnp.float32),
+            pltpu.VMEM((1, depth), jnp.float32),
+            pltpu.VMEM((1, HD), jnp.float32),
+            pltpu.VMEM((1, HD), jnp.float32),
+            dma((5,)),
             pltpu.VMEM((SLICES, rows, depth), jnp.bfloat16),
             pltpu.VMEM((rows, depth), jnp.bfloat16),
             pltpu.VMEM((depth, 3 * width), jnp.bfloat16),
@@ -424,9 +439,10 @@
             dma((W_MESSAGES,)), dma((W_MESSAGES,)),
         ],
         compiler_params=pltpu.CompilerParams(
-            vmem_limit_bytes=VMEM_LIMIT, collective_id=0, has_side_effects=True
+            vmem_limit_bytes=36 * MIB, collective_id=0, has_side_effects=True
         ),
-    )(tokens, mod_scale[None], shift[None], w, q_gain[None], k_gain[None], w_out)
+    )(*(pltpu.with_memory_space_constraint(one, pltpu.HBM) for one in
+        (tokens, mod_scale[None], shift[None], w, q_gain[None], k_gain[None], w_out)))
 
 
 def attention_kernel(heads, pat_ref, cnt_ref, t_ref, q_ref, kv_ref, out_ref, kwin, vwin, ones, acc, todo, sem):
@@ -540,7 +556,7 @@
             pltpu.SMEM((GS * 14,), jnp.int32),
             pltpu.SemaphoreType.DMA((6,)),
         ],
-        compiler_params=pltpu.CompilerParams(vmem_limit_bytes=VMEM_LIMIT),
+        compiler_params=pltpu.CompilerParams(vmem_limit_bytes=32 * MIB),
     )(pattern, counts, t.reshape(1), q, kv.reshape(3, GS, TILE, 2 * width))
 
 
@@ -698,7 +714,7 @@
         finish_kernel,
         name="finish",
         out_shape=jax.ShapeDtypeStruct((rows, depth), jnp.float32),
-        in_specs=[hbm, hbm, hbm],
+        in_specs=[hbm, pl.BlockSpec(memory_space=pltpu.HBM), hbm],
         out_specs=vmem,
         scratch_shapes=[
             pltpu.VMEM((SLICES // 2, rows, 2 * width), jnp.bfloat16),
@@ -706,7 +722,7 @@
             dma((SLICES,)), dma((SLICES,)), dma((8,)), dma((8,)), dma((8,)), dma((8,)), dma((16,)), dma(()),
         ],
         compiler_params=pltpu.CompilerParams(
-            vmem_limit_bytes=VMEM_LIMIT, collective_id=1, has_side_effects=True
+            vmem_limit_bytes=32 * MIB, collective_id=1, has_side_effects=True
         ),
     )(attn, w_out, wall)
 

time: 148 us -> 140 us (0.946)
  Pallas kernels: 145 us -> 138 us
  other arithmetic: 3 us -> 1.34 us
    pallas_call x1, Pallas kernels: 21.1 us -> 17.5 us  [attention(): pl.pallas_call(functools.partial(attention_kernel, heads), name='attentio...]
    pallas_call x1, Pallas kernels: 89.8 us -> 88 us  [gather_project(): pl.pallas_call(functools.partial(gather_kernel, heads), name='gather_proj...]
    convert_element_type x1, other arithmetic: 3 us -> 1.34 us  [per_device(): return (tokens.astype(jnp.float32) + gate * result).astype(jnp.bfloat16)]
where the time goes in v6:
time: 140 us
  Pallas kernels  138 us (99%)
    pallas_call x1, Pallas kernels, gather_project(): pl.pallas_call(functools.partial(gather_kernel, heads), name='gather_proj...  88 us
    pallas_call x1, Pallas kernels, finish(): pl.pallas_call(finish_kernel, name='finish', out_shape=jax.ShapeDtypeStru...  32.8 us
    pallas_call x1, Pallas kernels, attention(): pl.pallas_call(functools.partial(attention_kernel, heads), name='attentio...  17.5 us

profile of v6, /device:TPU:1, one launch (start us, length us, event | category | flops | bytes accessed | tf_op | source)
XLA Modules:
  0.0 139.8 jit_solution(5402141395353798437)
XLA Ops:
  0.0 0.0 copy-start.1
  0.0 0.0 copy-start.2
  0.0 88.0 %gather_project.1 = (bf16[1536,384]{1,0:T(8,128)(2,1)S(1)}, bf16[3,1536,768]{2,1,0:T(8,128)(2,1)S(1)}, bf16[4,2,2,4,48,3072]{5,4,3,2,1,0:T(8,128)(2,1)}) custom-call(bf16[192,3072]{1,0:T(8,128)(2,1)} %tok_hbm.1, f32[1,3072]{1,0:T(1,128)} %bitcast.12, f32[1,3072]{1,0:T(1,128)} %bitcast.13, bf16[3,3072,384]{2,1,0:T(8,128)(2,1)} %bitcast.11, ...), custom_call_target="tpu_custom_call" | custom-call | tf_op jit(solution)/shard_map/gather_project/pallas_call | solution.py:416
  88.0 0.0 copy-done.1
  88.0 0.0 copy-done.2
  88.0 0.0 copy-start
  88.0 17.5 %attention.1.attn = bf16[1536,384]{1,0:T(8,128)(2,1)S(1)} custom-call(s32[3,4,4]{2,1,0:T(4,128)S(1)} %copy-done.1, s32[8]{0:T(128)S(1)} %copy-done.2, s32[1]{0:T(128)} %bitcast.t_ref, bf16[1536,384]{1,0:T(8,128)(2,1)S(1)} %get-tuple-element.8.q_ref, bf16[3,4,384,768]{3,2,1,0:T(8,128)(2,1)S(1)} %bitcast.10), custom_call_target="tpu_custom_call" | custom-call | tf_op jit(solution)/shard_map/attention/pallas_call | solution.py:545
  105.5 0.0 copy-done
  105.5 0.0 copy-start.3
  105.6 0.0 copy-start.4
  105.6 32.8 %finish.1 = f32[192,3072]{1,0:T(8,128)S(1)} custom-call(bf16[1536,384]{1,0:T(8,128)(2,1)S(1)} %attention.1.attn, bf16[2,4,48,3072]{3,2,1,0:T(8,128)(2,1)S(1)} %bitcast.9, bf16[4,2,2,4,48,3072]{5,4,3,2,1,0:T(8,128)(2,1)} %get-tuple-element.10.wall), custom_call_target="tpu_custom_call" | custom-call | tf_op jit(solution)/shard_map/finish/pallas_call | solution.py:713
  138.4 0.0 copy-done.3
  138.4 0.0 copy-done.4
  138.4 1.3 add_convert_fusion
Async XLA Ops:
  0.0 88.0 %copy-start.1 = (s32[3,4,4]{2,1,0:T(4,128)S(1)}, s32[3,4,4]{2,1,0:T(4,128)}, u32[]{:S(2)}) copy-start(s32[3,4,4]{2,1,0:T(4,128)} %pat_ref.1) | copy-start | bytes 580
  0.0 88.0 %copy-start.2 = (s32[8]{0:T(128)S(1)}, s32[8]{0:T(128)}, u32[]{:S(2)}) copy-start(s32[8]{0:T(128)} %cnt_ref.1) | copy-start | bytes 100
  88.0 17.5 %copy-start = (bf16[384,3072]{1,0:T(8,128)(2,1)S(1)}, bf16[384,3072]{1,0:T(8,128)(2,1)}, u32[]{:S(2)}) copy-start(bf16[384,3072]{1,0:T(8,128)(2,1)} %param.17) | copy-start | bytes 7077892
  105.5 32.9 %copy-start.3 = (bf16[192,3072]{1,0:T(8,128)(2,1)S(1)}, bf16[192,3072]{1,0:T(8,128)(2,1)}, u32[]{:S(2)}) copy-start(bf16[192,3072]{1,0:T(8,128)(2,1)} %tok_hbm.1) | copy-start | bytes 3538948
  105.6 32.9 %copy-start.4 = (f32[3072]{0:T(1024)S(1)}, f32[3072]{0:T(1024)}, u32[]{:S(2)}) copy-start(f32[3072]{0:T(1024)} %param.13) | copy-start | bytes 36868

commit v7 on v6

--- a/solution.py
+++ b/solution.py
@@ -12,7 +12,7 @@
 HD = 128
 NT = 8
 ROWS = GS * TILE
-NONE = 3 * GS
+NONE = 9 * GS
 MIB = 1024 * 1024
 QSCALE = HD**-0.5 * 1.4426950408889634
 
@@ -445,27 +445,16 @@
         (tokens, mod_scale[None], shift[None], w, q_gain[None], k_gain[None], w_out)))
 
 
-def attention_kernel(heads, pat_ref, cnt_ref, t_ref, q_ref, kv_ref, out_ref, kwin, vwin, ones, acc, todo, sem):
+def attention_kernel(heads, pat_ref, cnt_ref, t_ref, q_ref, kv_ref, out_ref, ones, acc, todo):
     t = t_ref[0]
     width = heads * HD
     slots = (2 - t % 2, 0, 1 + t % 2)
-    copies = []
-    for o in range(3):
-        for part, into in ((0, kwin), (1, vwin)):
-            copy = pltpu.make_async_copy(
-                kv_ref.at[slots[o], :, :, part * width : (part + 1) * width],
-                into.at[o * GS : (o + 1) * GS],
-                sem.at[2 * o + part],
-            )
-            copy.start()
-            copies.append(copy)
-
     def list_tile(i, carry):
         count = jnp.int32(0)
         for o in range(3):
             inside = (t + o - 1 >= 0) & (t + o - 1 < NT)
             for j in range(GS):
-                todo[i * 14 + 1 + count] = o * GS + j
+                todo[i * 14 + 1 + count] = (o * 3 + slots[o]) * GS + j
                 live = inside & (pat_ref[o, i, j] > 0)
                 count = count + live.astype(jnp.int32)
         todo[i * 14 + 1 + count] = NONE
@@ -473,25 +462,15 @@
         return carry
 
     lax.fori_loop(0, GS, list_tile, 0)
-    kwin[NONE] = jnp.zeros_like(kwin[NONE])
-    vwin[NONE] = jnp.zeros_like(vwin[NONE])
     ones[3] = jnp.zeros_like(ones[3])
     place = lax.broadcasted_iota(jnp.int32, (TILE, HD), 0)
     for o in range(3):
         ones[o] = jnp.where(place < cnt_ref[jnp.clip(t + o - 1, 0, NT - 1)], 1.0, 0.0).astype(jnp.bfloat16)
-    for copy in copies:
-        copy.wait()
-
-    for o in range(3):
-        @pl.when(cnt_ref[jnp.clip(t + o - 1, 0, NT - 1)] < TILE)
-        def _():
-            def clear(j, carry):
-                for h in range(heads):
-                    cols = slice(h * HD, (h + 1) * HD)
-                    vwin[o * GS + j, :, cols] = vwin[o * GS + j, :, cols] * ones[o]
-                return carry
-
-            lax.fori_loop(0, GS, clear, 0)
+    def keys_of(one, cols):
+        return kv_ref[one // GS % 3, one % GS, :, cols]
+
+    def values_of(one, h):
+        return kv_ref[one // GS % 3, one % GS, :, width + h * HD : width + (h + 1) * HD] * ones[one // (3 * GS)]
 
     def tile(i, carry):
         mine = pl.ds(pl.multiple_of(i * TILE, TILE), TILE)
@@ -503,15 +482,14 @@
                 cols = slice(h * HD, (h + 1) * HD)
                 score = lax.dot_general(
                     q_ref[mine, cols],
-                    jnp.concatenate([kwin[one, :, cols] for one in which], axis=0),
+                    jnp.concatenate([keys_of(one, cols) for one in which], axis=0),
                     (((1,), (1,)), ((), ())),
                     preferred_element_type=jnp.float32,
                 )
                 probs.append(jnp.exp2(score).astype(jnp.bfloat16))
-            valid = jnp.concatenate([ones[one // GS] for one in which], axis=0)
+            valid = jnp.concatenate([ones[one // (3 * GS)] for one in which], axis=0)
             for h in range(heads):
-                cols = slice(h * HD, (h + 1) * HD)
-                values = jnp.concatenate([vwin[one, :, cols] for one in which], axis=0)
+                values = jnp.concatenate([values_of(one, h) for one in which], axis=0)
                 acc[h] += jnp.dot(
                     probs[h], jnp.concatenate([values, valid], axis=1), preferred_element_type=jnp.float32
                 )
@@ -540,21 +518,17 @@
     rows, width = q.shape
     heads = width // HD
     smem = pl.BlockSpec(memory_space=pltpu.SMEM)
-    hbm = pl.BlockSpec(memory_space=pl.ANY)
     vmem = pl.BlockSpec(memory_space=pltpu.VMEM)
     return pl.pallas_call(
         functools.partial(attention_kernel, heads),
         name="attention",
         out_shape=jax.ShapeDtypeStruct((rows, width), jnp.bfloat16),
-        in_specs=[smem, smem, smem, vmem, hbm],
+        in_specs=[smem, smem, smem, vmem, vmem],
         out_specs=vmem,
         scratch_shapes=[
-            pltpu.VMEM((NONE + 1, TILE, width), jnp.bfloat16),
-            pltpu.VMEM((NONE + 1, TILE, width), jnp.bfloat16),
             pltpu.VMEM((GS, TILE, HD), jnp.bfloat16),
             pltpu.VMEM((heads, TILE, 2 * HD), jnp.float32),
             pltpu.SMEM((GS * 14,), jnp.int32),
-            pltpu.SemaphoreType.DMA((6,)),
         ],
         compiler_params=pltpu.CompilerParams(vmem_limit_bytes=32 * MIB),
     )(pattern, counts, t.reshape(1), q, kv.reshape(3, GS, TILE, 2 * width))

time: 140 us -> 139 us (level)
  no operation moved by 1% of the time
where the time goes in v7:
time: 139 us
  Pallas kernels  137 us (99%)
    pallas_call x1, Pallas kernels, gather_project(): pl.pallas_call(functools.partial(gather_kernel, heads), name='gather_proj...  88 us
    pallas_call x1, Pallas kernels, finish(): pl.pallas_call(finish_kernel, name='finish', out_shape=jax.ShapeDtypeStru...  32.4 us
    pallas_call x1, Pallas kernels, attention(): pl.pallas_call(functools.partial(attention_kernel, heads), name='attentio...  16.9 us

profile of v7, /device:TPU:1, one launch (start us, length us, event | category | flops | bytes accessed | tf_op | source)
XLA Modules:
  0.0 138.7 jit_solution(13068728583284238407)
XLA Ops:
  0.0 0.0 copy-start.1
  0.0 0.0 copy-start.2
  0.0 88.0 %gather_project.1 = (bf16[1536,384]{1,0:T(8,128)(2,1)S(1)}, bf16[3,1536,768]{2,1,0:T(8,128)(2,1)S(1)}, bf16[4,2,2,4,48,3072]{5,4,3,2,1,0:T(8,128)(2,1)}) custom-call(bf16[192,3072]{1,0:T(8,128)(2,1)} %tok_hbm.1, f32[1,3072]{1,0:T(1,128)} %bitcast.12, f32[1,3072]{1,0:T(1,128)} %bitcast.13, bf16[3,3072,384]{2,1,0:T(8,128)(2,1)} %bitcast.11, ...), custom_call_target="tpu_custom_call" | custom-call | tf_op jit(solution)/shard_map/gather_project/pallas_call | solution.py:416
  88.0 0.0 copy-done.1
  88.0 0.0 copy-done.2
  88.0 0.0 copy-start
  88.0 16.9 %attention.1.attn = bf16[1536,384]{1,0:T(8,128)(2,1)S(1)} custom-call(s32[3,4,4]{2,1,0:T(4,128)S(1)} %copy-done.1, s32[8]{0:T(128)S(1)} %copy-done.2, s32[1]{0:T(128)} %bitcast.t_ref, bf16[1536,384]{1,0:T(8,128)(2,1)S(1)} %get-tuple-element.8.q_ref, bf16[3,4,384,768]{3,2,1,0:T(8,128)(2,1)S(1)} %bitcast.10), custom_call_target="tpu_custom_call" | custom-call | tf_op jit(solution)/shard_map/attention/pallas_call | solution.py:522
  104.9 0.0 copy-done
  104.9 0.0 copy-start.3
  104.9 0.0 copy-start.4
  105.0 32.4 %finish.1 = f32[192,3072]{1,0:T(8,128)S(1)} custom-call(bf16[1536,384]{1,0:T(8,128)(2,1)S(1)} %attention.1.attn, bf16[2,4,48,3072]{3,2,1,0:T(8,128)(2,1)S(1)} %bitcast.9, bf16[4,2,2,4,48,3072]{5,4,3,2,1,0:T(8,128)(2,1)} %get-tuple-element.10.wall), custom_call_target="tpu_custom_call" | custom-call | tf_op jit(solution)/shard_map/finish/pallas_call | solution.py:687
  137.3 0.0 copy-done.3
  137.3 0.0 copy-done.4
  137.4 1.3 add_convert_fusion
Async XLA Ops:
  0.0 88.0 %copy-start.1 = (s32[3,4,4]{2,1,0:T(4,128)S(1)}, s32[3,4,4]{2,1,0:T(4,128)}, u32[]{:S(2)}) copy-start(s32[3,4,4]{2,1,0:T(4,128)} %pat_ref.1) | copy-start | bytes 580
  0.0 88.0 %copy-start.2 = (s32[8]{0:T(128)S(1)}, s32[8]{0:T(128)}, u32[]{:S(2)}) copy-start(s32[8]{0:T(128)} %cnt_ref.1) | copy-start | bytes 100
  88.0 16.9 %copy-start = (bf16[384,3072]{1,0:T(8,128)(2,1)S(1)}, bf16[384,3072]{1,0:T(8,128)(2,1)}, u32[]{:S(2)}) copy-start(bf16[384,3072]{1,0:T(8,128)(2,1)} %param.17) | copy-start | bytes 7077892
  104.9 32.4 %copy-start.3 = (bf16[192,3072]{1,0:T(8,128)(2,1)S(1)}, bf16[192,3072]{1,0:T(8,128)(2,1)}, u32[]{:S(2)}) copy-start(bf16[192,3072]{1,0:T(8,128)(2,1)} %tok_hbm.1) | copy-start | bytes 3538948
  104.9 32.4 %copy-start.4 = (f32[3072]{0:T(1024)S(1)}, f32[3072]{0:T(1024)}, u32[]{:S(2)}) copy-start(f32[3072]{0:T(1024)} %param.13) | copy-start | bytes 36868

commit v8 on v7

--- a/solution.py
+++ b/solution.py
@@ -277,7 +277,7 @@
 
     def last_chunk(k):
         def handler():
-            if k == 0:
+            if k == 1:
                 w_half(0)
             for dy, number in last:
                 arrive(number, k, slot_of(dy, 1))

time: 139 us -> 138 us (level)
  no operation moved by 1% of the time
where the time goes in v8:
time: 138 us; the launch traced here: 139 us
  Pallas kernels  137 us (99%)
    pallas_call x1, Pallas kernels, gather_project(): pl.pallas_call(functools.partial(gather_kernel, heads), name='gather_proj...  88 us
    pallas_call x1, Pallas kernels, finish(): pl.pallas_call(finish_kernel, name='finish', out_shape=jax.ShapeDtypeStru...  32.4 us
    pallas_call x1, Pallas kernels, attention(): pl.pallas_call(functools.partial(attention_kernel, heads), name='attentio...  17.1 us

profile of v8, /device:TPU:1, one launch (start us, length us, event | category | flops | bytes accessed | tf_op | source)
XLA Modules:
  0.0 138.9 jit_solution(14062027691126922977)
XLA Ops:
  0.0 0.0 copy-start.1
  0.0 0.0 copy-start.2
  0.0 88.0 %gather_project.1 = (bf16[1536,384]{1,0:T(8,128)(2,1)S(1)}, bf16[3,1536,768]{2,1,0:T(8,128)(2,1)S(1)}, bf16[4,2,2,4,48,3072]{5,4,3,2,1,0:T(8,128)(2,1)}) custom-call(bf16[192,3072]{1,0:T(8,128)(2,1)} %tok_hbm.1, f32[1,3072]{1,0:T(1,128)} %bitcast.12, f32[1,3072]{1,0:T(1,128)} %bitcast.13, bf16[3,3072,384]{2,1,0:T(8,128)(2,1)} %bitcast.11, ...), custom_call_target="tpu_custom_call" | custom-call | tf_op jit(solution)/shard_map/gather_project/pallas_call | solution.py:416
  88.0 0.0 copy-done.1
  88.0 0.0 copy-done.2
  88.0 0.0 copy-start
  88.0 17.1 %attention.1.attn = bf16[1536,384]{1,0:T(8,128)(2,1)S(1)} custom-call(s32[3,4,4]{2,1,0:T(4,128)S(1)} %copy-done.1, s32[8]{0:T(128)S(1)} %copy-done.2, s32[1]{0:T(128)} %bitcast.t_ref, bf16[1536,384]{1,0:T(8,128)(2,1)S(1)} %get-tuple-element.8.q_ref, bf16[3,4,384,768]{3,2,1,0:T(8,128)(2,1)S(1)} %bitcast.10), custom_call_target="tpu_custom_call" | custom-call | tf_op jit(solution)/shard_map/attention/pallas_call | solution.py:522
  105.1 0.0 copy-done
  105.1 0.0 copy-start.3
  105.2 0.0 copy-start.4
  105.2 32.4 %finish.1 = f32[192,3072]{1,0:T(8,128)S(1)} custom-call(bf16[1536,384]{1,0:T(8,128)(2,1)S(1)} %attention.1.attn, bf16[2,4,48,3072]{3,2,1,0:T(8,128)(2,1)S(1)} %bitcast.9, bf16[4,2,2,4,48,3072]{5,4,3,2,1,0:T(8,128)(2,1)} %get-tuple-element.10.wall), custom_call_target="tpu_custom_call" | custom-call | tf_op jit(solution)/shard_map/finish/pallas_call | solution.py:687
  137.5 0.0 copy-done.3
  137.5 0.0 copy-done.4
  137.6 1.3 add_convert_fusion
Async XLA Ops:
  0.0 88.0 %copy-start.1 = (s32[3,4,4]{2,1,0:T(4,128)S(1)}, s32[3,4,4]{2,1,0:T(4,128)}, u32[]{:S(2)}) copy-start(s32[3,4,4]{2,1,0:T(4,128)} %pat_ref.1) | copy-start | bytes 580
  0.0 88.0 %copy-start.2 = (s32[8]{0:T(128)S(1)}, s32[8]{0:T(128)}, u32[]{:S(2)}) copy-start(s32[8]{0:T(128)} %cnt_ref.1) | copy-start | bytes 100
  88.0 17.1 %copy-start = (bf16[384,3072]{1,0:T(8,128)(2,1)S(1)}, bf16[384,3072]{1,0:T(8,128)(2,1)}, u32[]{:S(2)}) copy-start(bf16[384,3072]{1,0:T(8,128)(2,1)} %param.17) | copy-start | bytes 7077892
  105.1 32.4 %copy-start.3 = (bf16[192,3072]{1,0:T(8,128)(2,1)S(1)}, bf16[192,3072]{1,0:T(8,128)(2,1)}, u32[]{:S(2)}) copy-start(bf16[192,3072]{1,0:T(8,128)(2,1)} %tok_hbm.1) | copy-start | bytes 3538948
  105.2 32.4 %copy-start.4 = (f32[3072]{0:T(1024)S(1)}, f32[3072]{0:T(1024)}, u32[]{:S(2)}) copy-start(f32[3072]{0:T(1024)} %param.13) | copy-start | bytes 36868
